TPU v7x, 128 devices: a whole 4x4x4 slice. The times are simulated.
128 devices in a mesh: dp: 16 (over z, x), tp: 8 (over y, core).
Axes of the slice: x: 4, y: 4, z: 4, core: 2. Of those that a mesh axis runs over, the one named last changes fastest.
Arguments:
- attn_out: bfloat16 [16384, 4096], P('dp', 'tp'), may hold values from -6 to 6
- residual_in: bfloat16 [16384, 5120], P('dp', 'tp'), may hold values from -6 to 6
- teacher: bfloat16 [16384, 5120], P('dp', 'tp'), may hold values from -6 to 6
- out_weight: bfloat16 [4096, 5120], P(None, 'tp'), may hold values from -0.09375 to 0.09375
- error_buf: bfloat16 [16, 4096, 5120], P('dp', None, 'tp'), may hold values from -6 to 6
- q_start: float32 [5120, 64], P('tp'), may hold values from -6 to 6
Outputs:
- error_next: bfloat16 [16, 4096, 5120], P('dp', None, 'tp')
- q_next: float32 [5120, 64], P('tp')
All inputs are finite; a program needn't handle non-finite values.
Results may differ from a plain program's by a relative error of at most 0.015.
Values may be sent and summed in bfloat16 or wider, within the bound.
A program may use at most 128 MiB of HBM per device.

v0:
```python
import jax
import jax.numpy as jnp
from jax import lax
from jax.sharding import PartitionSpec as P


def orthonormal_rows(factor, gram_matrix):
    lower_factor = jnp.linalg.cholesky(gram_matrix)
    return lax.linalg.triangular_solve(
        lower_factor, factor, left_side=False, lower=True, transpose_a=True
    )


def per_device(attn_out, residual_in, teacher, out_weight, error_buf, q_start):
    replicas = lax.axis_size("dp")
    heads_full = lax.all_gather(attn_out, "tp", axis=1, tiled=True)
    projected = jnp.dot(heads_full, out_weight, preferred_element_type=jnp.float32)
    diff = (residual_in.astype(jnp.float32) + projected - teacher.astype(jnp.float32)).astype(
        jnp.bfloat16
    )
    grad = lax.dot_general(
        heads_full, diff, (((0,), (0,)), ((), ())), preferred_element_type=jnp.float32
    )
    scale_factor = 1.0 / jnp.sqrt(jnp.float32(attn_out.shape[0]))
    matrix = grad * scale_factor + error_buf[0].astype(jnp.float32)
    left_part = jnp.dot(matrix, q_start, precision=lax.Precision.HIGHEST)
    left_sum = lax.psum(left_part, ("dp", "tp")) / replicas
    gram_matrix = jnp.dot(left_sum.T, left_sum, precision=lax.Precision.HIGHEST)
    basis = orthonormal_rows(left_sum, gram_matrix)
    right_part = lax.dot_general(
        matrix, basis, (((0,), (0,)), ((), ())), precision=lax.Precision.HIGHEST
    )
    q_next = lax.psum(right_part.astype(jnp.bfloat16), "dp").astype(jnp.float32) / replicas
    approx = jnp.dot(basis, q_next.T, precision=lax.Precision.HIGHEST)
    error_next = (matrix - approx).astype(jnp.bfloat16)[None]
    return (error_next, q_next)


def solution(mesh):
    return jax.shard_map(
        per_device,
        mesh=mesh,
        in_specs=(
            P("dp", "tp"),
            P("dp", "tp"),
            P("dp", "tp"),
            P(None, "tp"),
            P("dp", None, "tp"),
            P("tp", None),
        ),
        out_specs=(P("dp", None, "tp"), P("tp", None)),
        check_vma=False,
    )
```

profile of v0, /device:TPU:0, one launch (start us, length us, event | category | flops | bytes accessed | tf_op | source)
XLA Modules:
  0.0 377.0 jit_solution(9335755918249297134)
XLA Ops:
  7.2 0.0 copy-start
  7.2 0.0 all-gather.2.cloned.1.call-start
  7.2 0.7 all-gather.2.cloned.1.call-update
  7.9 0.0 copy-start.5
  7.9 0.0 all-reduce.3.cloned.1.call-start
  8.0 8.0 %copy.8 = bf16[1,4096,640]{1,2,0:T(8,128)(2,1)} copy(bf16[1,4096,640]{2,1,0:T(8,128)(2,1)} %param.10) | data formatting | bytes 10485760 | tf_op args[4]
  16.0 45.9 %all-gather.2.cloned.1.call-done = bf16[1024,4096]{1,0:T(8,128)(2,1)} async-done(((bf16[1024,512]{1,0:T(8,128)(2,1)}), bf16[1024,4096]{1,0:T(8,128)(2,1)}) %all-gather.2.cloned.1.call-update) | async-done | bytes 8388624 | tf_op jit(solution)/shard_map/all_gather | solution.py:16
  61.9 11.0 %subtract_convert_fusion.1 = bf16[1024,640]{1,0:T(8,128)(2,1)S(1)} fusion(bf16[1024,640]{1,0:T(8,128)(2,1)S(1)} %copy-done.5, bf16[1024,640]{1,0:T(8,128)(2,1)S(1)} %copy-done.6, bf16[1024,4096]{1,0:T(8,128)(2,1)} %all-gather.2.cloned.1.call-done, bf16[4096,640]{1,0:T(8,128)(2,1)} %param.9), kind=kOutput, calls=%fused_computation.3 | convolution fusion | flops 5371985920 | bytes 17563648 | tf_op jit(solution)/shard_map/dot_general | solution.py:17
  72.9 0.0 copy-done.2
  72.9 0.0 copy-done.3
  73.0 5.9 %convert_add_fusion = f32[4096,640]{0,1:T(8,128)S(1)} fusion(bf16[1024,640]{1,0:T(8,128)(2,1)S(1)} %subtract_convert_fusion.1, bf16[1024,4096]{1,0:T(8,128)(2,1)S(1)} %copy-done.3, bf16[1,4096,640]{1,2,0:T(8,128)(2,1)S(1)} %copy-done.2), kind=kOutput, calls=%fused_computation | convolution fusion | flops 5376573440 | bytes 25427968 | tf_op jit(solution)/shard_map/dot_general | solution.py:21
  78.9 4.0 %copy-done.1 = f32[4096,640]{0,1:T(8,128)} copy-done((f32[4096,640]{0,1:T(8,128)}, f32[4096,640]{0,1:T(8,128)S(1)}, u32[]{:S(2)}) %copy-start.1) | copy-done | bytes 10485784
  82.8 0.0 copy-done
  82.8 7.8 %fusion.12 = f32[4096,64]{0,1:T(8,128)} fusion(f32[4096,640]{0,1:T(8,128)S(1)} %convert_add_fusion, f32[640,64]{0,1:T(8,128)S(1)} %copy-done), kind=kOutput, calls=%fused_computation.23 | convolution fusion | flops 2013265920 | bytes 11698176 | tf_op jit(solution)/shard_map/dot_general | solution.py:26
  90.7 0.0 all-reduce.3.cloned.1.call-update
  90.7 0.3 all-reduce.5.cloned.1.call-start
  91.0 146.8 %all-reduce.3.cloned.1.call-done = f32[4096,64]{0,1:T(8,128)} async-done(((f32[4096,64]{0,1:T(8,128)}), f32[4096,64]{0,1:T(8,128)}) %all-reduce.3.cloned.1.call-update) | async-done | bytes 1048592 | tf_op jit(solution)/shard_map/psum | solution.py:27
  237.7 2.6 fusion.3
  240.3 0.1 copy.9
  240.4 5.8 %cholesky.16 = f32[64,64]{1,0:T(8,128)S(1)} custom-call(f32[64,64]{1,0:T(8,128)S(1)} %fusion.9), custom_call_target="Cholesky" | custom-call | tf_op jit(solution)/shard_map/jit(cholesky)/cholesky | solution.py:8
  246.3 0.6 compare_reduce_fusion
  246.9 0.7 fusion.7
  247.6 4.9 %custom-call.6 = f32[1,64,64]{1,2,0:T(8,128)S(1)} custom-call(f32[1,64,64]{2,1,0:T(8,128)S(1)} %fusion.7), custom_call_target="InvertDiagBlocksLowerTriangular" | custom-call | tf_op jit(solution)/shard_map/triangular_solve | solution.py:9
  252.5 2.3 fusion.1
  254.8 13.4 %convolution_convert_fusion = bf16[640,64]{0,1:T(8,128)(2,1)} fusion(f32[4096,640]{0,1:T(8,128)} %copy-done.1, f32[4096,64]{0,1:T(8,128)S(1)} %fusion.1), kind=kOutput, calls=%fused_computation.4 | convolution fusion | flops 2013306880 | bytes 11616256 | tf_op jit(solution)/shard_map/dot_general | solution.py:30
  268.3 0.0 all-reduce.5.cloned.1.call-update
  268.3 80.5 %all-reduce.5.cloned.1.call-done = bf16[640,64]{0,1:T(8,128)(2,1)} async-done(((bf16[640,64]{0,1:T(8,128)(2,1)}), bf16[640,64]{0,1:T(8,128)(2,1)}) %all-reduce.5.cloned.1.call-update) | async-done | bytes 81936 | tf_op jit(solution)/shard_map/psum | solution.py:33
  348.8 0.9 convert_multiply_fusion
  349.7 0.0 copy-start.4
  349.7 13.0 %fusion = bf16[1,4096,640]{1,2,0:T(8,128)(2,1)} fusion(f32[4096,640]{0,1:T(8,128)} %copy-done.1, f32[4096,64]{0,1:T(8,128)S(1)} %fusion.1, f32[640,64]{0,1:T(8,128)S(1)} %convert_multiply_fusion), kind=kOutput, calls=%fused_computation.2 | convolution fusion | flops 2018508800 | bytes 16941056 | tf_op jit(solution)/shard_map/dot_general | solution.py:34
  362.7 0.0 copy-done.4
  362.7 7.8 %copy.11 = bf16[1,4096,640]{2,1,0:T(8,128)(2,1)} copy(bf16[1,4096,640]{1,2,0:T(8,128)(2,1)} %fusion) | data formatting | bytes 10485760
  (8 shorter events, 0.1 us)
Async XLA Ops:
  7.2 75.7 %copy-start = (f32[640,64]{0,1:T(8,128)S(1)}, f32[640,64]{0,1:T(8,128)}, u32[]{:S(2)}) copy-start(f32[640,64]{0,1:T(8,128)} %param.11) | copy-start | bytes 491524
  7.2 54.7 %all-gather.2.cloned.1.call-start = ((), (), s32[]{:S(2)}) async-start(), calls=%async_computation | async-start | bytes 9437184 | tf_op jit(solution)/shard_map/all_gather | solution.py:16
  7.9 54.0 %copy-start.5 = (bf16[1024,640]{1,0:T(8,128)(2,1)S(1)}, bf16[1024,640]{1,0:T(8,128)(2,1)}, u32[]{:S(2)}) copy-start(bf16[1024,640]{1,0:T(8,128)(2,1)} %param.8) | copy-start | bytes 3932164
  7.9 54.0 %copy-start.6 = (bf16[1024,640]{1,0:T(8,128)(2,1)S(1)}, bf16[1024,640]{1,0:T(8,128)(2,1)}, u32[]{:S(2)}) copy-start(bf16[1024,640]{1,0:T(8,128)(2,1)} %param.7) | copy-start | bytes 3932164
  7.9 229.8 %all-reduce.3.cloned.1.call-start = ((), (), s32[]{:S(2)}) async-start(), calls=%async_computation.1 | async-start | bytes 2097152 | tf_op jit(solution)/shard_map/psum | solution.py:27
  61.9 11.0 %copy-start.2 = (bf16[1,4096,640]{1,2,0:T(8,128)(2,1)S(1)}, bf16[1,4096,640]{1,2,0:T(8,128)(2,1)}, u32[]{:S(2)}) copy-start(bf16[1,4096,640]{1,2,0:T(8,128)(2,1)} %copy.8) | copy-start | bytes 15728644
  61.9 11.0 %copy-start.3 = (bf16[1024,4096]{1,0:T(8,128)(2,1)S(1)}, bf16[1024,4096]{1,0:T(8,128)(2,1)}, u32[]{:S(2)}) copy-start(bf16[1024,4096]{1,0:T(8,128)(2,1)} %all-gather.2.cloned.1.call-done) | copy-start | bytes 25165828
  78.9 4.0 %copy-start.1 = (f32[4096,640]{0,1:T(8,128)}, f32[4096,640]{0,1:T(8,128)S(1)}, u32[]{:S(2)}) copy-start(f32[4096,640]{0,1:T(8,128)S(1)} %convert_add_fusion) | copy-start | bytes 31457284
  90.7 258.1 %all-reduce.5.cloned.1.call-start = ((), (), s32[]{:S(2)}) async-start(), calls=%async_computation.2 | async-start | bytes 163840 | tf_op jit(solution)/shard_map/psum | solution.py:33
  349.7 13.0 %copy-start.4 = (f32[640,64]{0,1:T(8,128)}, f32[640,64]{0,1:T(8,128)S(1)}, u32[]{:S(2)}) copy-start(f32[640,64]{0,1:T(8,128)S(1)} %convert_multiply_fusion) | copy-start | bytes 491524
Sparse Core Ops, SparseCore 0:
  9.7 52.1 all-gather.1
  90.8 146.8 all-reduce.2
  268.4 80.3 all-reduce.4
where the time goes:
time: 378 us; the launch traced here: 377 us
  waiting for transfers between devices  274 us (72%)
  matrix products  56.1 us (15%)
  local copies, waits for them, and re-layouts  19.9 us (5%)
  between operations  13.9 us (4%)
  other arithmetic  13 us (3%)
    psum x1, waiting for transfers between devices, per_device(): left_sum = lax.psum(left_part, ('dp', 'tp')) / replicas  147 us
    psum x1, waiting for transfers between devices, per_device(): lax.psum(right_part.astype(jnp.bfloat16), 'dp').astype(jnp.float32)  80.5 us
    all_gather x1, waiting for transfers between devices, per_device(): heads_full = lax.all_gather(attn_out, 'tp', axis=1, tiled=True)  45.9 us
    unnamed x16, local copies, waits for them, and re-layouts  19.8 us
    dot_general x1, matrix products, per_device(): lax.dot_general(matrix, basis, (((0,), (0,)), ((), ())), precision=lax.Pr...  13.4 us
    dot_general x1, matrix products, per_device(): approx = jnp.dot(basis, q_next.T, precision=lax.Precision.HIGHEST)  13 us
    dot_general x1, matrix products, per_device(): jnp.dot(heads_full, out_weight, preferred_element_type=jnp.float32)  11 us
    dot_general x1, matrix products, per_device(): left_part = jnp.dot(matrix, q_start, precision=lax.Precision.HIGHEST)  7.82 us
  transfers between devices with their start and end apart: 3, of which 3 were waited for; matrix products, arithmetic and copies ran while one was open for 2% of the time, Pallas kernels for 0%

commit v1 on v0

v1 whole, which is shorter than its diff:
```python
import jax
import jax.numpy as jnp
from jax import lax
from jax.experimental import pallas as pl
from jax.experimental.pallas import tpu as pltpu
from jax.sharding import PartitionSpec as P

MESH = pl.DeviceIdType.MESH
F32, BF16 = jnp.float32, jnp.bfloat16
DP, TP = 16, 8
TOK, FEAT, COLS, RANK = 1024, 512, 640, 64
ROWS = FEAT * TP
PIECE = FEAT // DP
TOKP = TOK // TP
HALF = TOK // 2
CUTS = 2
CUT = HALF // CUTS
TILES = 48


def dot(a, b):
    return jnp.dot(a, b, preferred_element_type=F32)


def fold(x):
    return x + pltpu.roll(x, RANK, 1)


def split(x):
    lane = lax.broadcasted_iota(jnp.int32, x.shape, 1)
    high = x.astype(BF16).astype(F32)
    return jnp.where(lane < RANK, high, x - high).astype(BF16)


def split_rows(x):
    high = x.astype(BF16).astype(F32)
    low = x - high
    return (
        jnp.concatenate([high, high], axis=0).astype(BF16),
        jnp.concatenate([low, low], axis=0).astype(BF16),
    )


def inverse_factor(gram):
    lane = lax.broadcasted_iota(jnp.int32, (8, 128), 1)
    sub = lax.broadcasted_iota(jnp.int32, (8, 128), 0)
    blocks = []
    for b in range(8):
        eye = jnp.where(lane == sub + (RANK + 8 * b), 1.0, 0.0)
        blocks.append(jnp.where(lane < RANK, gram[8 * b : 8 * b + 8, :], eye))
    for k in range(RANK):
        home, at = k // 8, k % 8
        pivot = jnp.broadcast_to(blocks[home][at : at + 1, :], (8, 128))
        scaled = pivot / jnp.broadcast_to(pivot[:, k : k + 1], (8, 128))
        for b in range(home, 8):
            column = jnp.broadcast_to(blocks[b][:, k : k + 1], (8, 128))
            if b == home:
                column = jnp.where(sub > at, column, 0.0)
            blocks[b] = blocks[b] - column * scaled
    out = []
    for b in range(8):
        diagonal = jnp.sum(jnp.where(lane == sub + 8 * b, blocks[b], 0.0), axis=1, keepdims=True)
        rows = jnp.where(lane < RANK, 0.0, blocks[b] * lax.rsqrt(diagonal))
        out.append(fold(rows))
    return jnp.concatenate(out, axis=0)


def main_kernel(
    a_hbm, res_hbm, tch_hbm, w_hbm, e_hbm, qt_ref,
    m_hbm, phat_ref, qnext_ref,
    abuf, at, wv, ev, res, tch, proj, wblk, qcat, xq,
    wq_send, wq_recv, wq_full, dq_send, dq_recv, dq_full,
    pa_send, pa_recv, eq_send, e_recv, e2_send, e2_recv, pfull, pt,
    r_send, r_recv, r_full,
    load_sem, ag_send, ag_recv, x_send, x_recv, out_sem,
):
    d, t = lax.axis_index("dp"), lax.axis_index("tp")
    y, c = t // 2, lax.rem(t, 2)
    sib = y * 2 + 1 - c
    up = lax.rem(y + 1, 4) * 2 + c
    down = lax.rem(y + 3, 4) * 2 + c
    far = lax.rem(y + 2, 4) * 2 + c

    def other(owner):
        return (owner // 2) * 2 + 1 - lax.rem(owner, 2)

    load_blk = pltpu.make_async_copy(w_hbm.at[:, pl.ds(pl.multiple_of(d * PIECE, PIECE), PIECE)], wblk, load_sem.at[0])
    load_a = pltpu.make_async_copy(a_hbm, abuf.at[t], load_sem.at[1])
    load_e = pltpu.make_async_copy(e_hbm, ev, load_sem.at[2])
    load_res = pltpu.make_async_copy(res_hbm, res, load_sem.at[3])
    load_tch = pltpu.make_async_copy(tch_hbm, tch, load_sem.at[4])
    load_w = pltpu.make_async_copy(w_hbm, wv, load_sem.at[5])
    for load in (load_blk, load_a, load_e, load_res, load_tch, load_w):
        load.start()

    barrier = pltpu.get_barrier_semaphore()

    @pl.loop(1, TP)
    def _(k):
        pl.semaphore_signal(barrier, inc=1, device_id={"tp": lax.rem(t + k, TP)}, device_id_type=MESH)

    @pl.loop(1, DP)
    def _(k):
        pl.semaphore_signal(barrier, inc=1, device_id={"dp": lax.rem(d + k, DP)}, device_id_type=MESH)

    q = qt_ref[...]
    high = q.astype(BF16).astype(F32)
    qcat[...] = jnp.concatenate([high, q - high], axis=0).T.astype(BF16)

    load_blk.wait()
    part = dot(wblk[...].reshape(TP * PIECE, COLS), qcat[...])
    wq_send[...] = split(fold(part)).reshape(TP, PIECE, 128)
    wq_recv[t] = wq_send[t]

    pl.semaphore_wait(barrier, TP - 1 + DP - 1)

    def send_tp(i, src, dst):
        @pl.loop(1, TP)
        def _(k):
            peer = lax.rem(t + k, TP)
            pltpu.make_async_remote_copy(
                src(peer), dst, x_send.at[i], x_recv.at[i], device_id={"tp": peer}, device_id_type=MESH
            ).start()

    def send_dp(i, src, dst):
        @pl.loop(1, DP)
        def _(k):
            peer = lax.rem(d + k, DP)
            pltpu.make_async_remote_copy(
                src(peer), dst, x_send.at[i], x_recv.at[i], device_id={"dp": peer}, device_id_type=MESH
            ).start()

    def wait_all(sems, i, like):
        pltpu.make_async_copy(like, like, sems.at[i]).wait()

    sends = []

    def rows(h, i):
        return pl.ds(h * HALF + i * CUT, CUT)

    def ag(owner, h, i, dest, src=None):
        r = rows(h, i)
        copy = pltpu.make_async_remote_copy(
            abuf.at[owner, r] if src is None else src.at[r], abuf.at[owner, r],
            ag_send.at[len(sends)], ag_recv.at[owner, h, i],
            device_id={"tp": dest}, device_id_type=MESH,
        )
        copy.start()
        sends.append(copy)

    def arrived(owner, h, i):
        r = rows(h, i)
        pltpu.make_async_copy(abuf.at[owner, r], abuf.at[owner, r], ag_recv.at[owner, h, i]).wait()

    send_tp(0, lambda peer: wq_send.at[peer], wq_recv.at[t])
    for hh in range(2):
        for i in range(CUTS):
            ag(t, hh, i, up, a_hbm)
            ag(t, 1 - hh, i, down, a_hbm)
    for h in range(2):
        for i in range(CUTS):
            ag(t, h, i, sib, a_hbm)

    load_e.wait()

    @pl.loop(0, TP)
    def _(k):
        block = ev[pl.ds(pl.multiple_of(k * FEAT, FEAT), FEAT), :]
        eq_send[k] = split(fold(dot(block, qcat[...])))

    mine = pl.ds(pl.multiple_of(d * PIECE, PIECE), PIECE)

    def piece(peer):
        return pl.ds(pl.multiple_of(peer * PIECE, PIECE), PIECE)

    e_recv[d] = eq_send[:, mine, :]
    send_dp(1, lambda peer: eq_send.at[:, piece(peer)], e_recv.at[d])

    wait_all(x_recv, 0, wq_recv.at[pl.ds(0, TP - 1)])
    total = wq_recv[0].astype(F32)
    for k in range(1, TP):
        total += wq_recv[k].astype(F32)
    wq_full[mine, :] = split(fold(total))
    send_dp(2, lambda peer: wq_full.at[mine], wq_full.at[mine])

    load_res.wait()
    load_tch.wait()
    STEP = 256

    @pl.loop(0, TOK // STEP)
    def _(k):
        r = pl.ds(pl.multiple_of(k * STEP, STEP), STEP)
        xq[r, :] = dot(res[r, :], qcat[...]) - dot(tch[r, :], qcat[...])

    load_a.wait()
    load_w.wait()

    def take(owner, lo, n, first=False):
        @pl.loop(0, n // STEP)
        def _(k):
            r = pl.ds(pl.multiple_of(lo + k * STEP, STEP), STEP)
            block = abuf[owner, r, :]
            at[owner, :, r] = block.T
            term = dot(block, wv[owner])
            if first:
                proj[r, :] = term
            else:
                proj[r, :] += term

    take(t, 0, TOK, first=True)

    wait_all(x_recv, 2, wq_full.at[pl.ds(0, FEAT - PIECE)])

    @pl.loop(0, TOK // STEP)
    def _(k):
        r = pl.ds(pl.multiple_of(k * STEP, STEP), STEP)
        part = xq[r, :] + dot(abuf[t, r, :], wq_full[...])
        dq_send[r, :] = split(fold(part))

    def tokens(peer):
        return pl.ds(pl.multiple_of(peer * TOKP, TOKP), TOKP)

    dq_recv[t] = dq_send[tokens(t), :]
    send_tp(3, lambda peer: dq_send.at[tokens(peer)], dq_recv.at[t])

    for h in range(2):
        for i in range(CUTS):
            arrived(sib, h, i)
    take(sib, 0, TOK)

    wait_all(x_recv, 3, dq_recv.at[pl.ds(0, TP - 1)])
    total = dq_recv[0].astype(F32)
    for k in range(1, TP):
        total += dq_recv[k].astype(F32)
    dq_full[tokens(t), :] = split(fold(total))
    send_tp(4, lambda peer: dq_full.at[tokens(t)], dq_full.at[tokens(t)])

    for i in range(CUTS):
        arrived(down, 0, i)
        ag(down, 0, i, up)
        ag(down, 0, i, sib)
        arrived(up, 1, i)
        ag(up, 1, i, down)
        ag(up, 1, i, sib)

    wait_all(x_recv, 1, e_recv.at[pl.ds(0, DP - 1)])

    @pl.loop(0, TP)
    def _(k):
        total = e_recv[0, k].astype(F32)
        for j in range(1, DP):
            total += e_recv[j, k].astype(F32)
        e2_send[k] = split(fold(total))

    e2_recv[t] = e2_send[t]
    send_tp(5, lambda peer: e2_send.at[peer], e2_recv.at[t])

    wait_all(x_recv, 4, dq_full.at[pl.ds(0, TOK - TOKP)])
    part = dot(at[t], dq_full[...]) * (1.0 / 32.0)
    pa_send[...] = split(fold(part))
    pa_recv[d] = pa_send[mine, :]
    send_dp(6, lambda peer: pa_send.at[piece(peer)], pa_recv.at[d])

    take(down, 0, HALF)
    take(up, HALF, HALF)

    wait_all(x_recv, 5, e2_recv.at[pl.ds(0, TP - 1)])
    wait_all(x_recv, 6, pa_recv.at[pl.ds(0, DP - 1)])
    total = e2_recv[0].astype(F32)
    for k in range(1, TP):
        total += e2_recv[k].astype(F32)
    for k in range(DP):
        total += pa_recv[k].astype(F32)
    pfull[t, mine, :] = split(fold(total) * (1.0 / DP))
    send_tp(7, lambda peer: pfull.at[t, mine], pfull.at[t, mine])

    for i in range(CUTS):
        arrived(down, 1, i)
        ag(down, 1, i, sib)
        arrived(up, 0, i)
        ag(up, 0, i, sib)

    wait_all(x_recv, 7, pfull.at[0, pl.ds(0, (TP - 1) * PIECE)])
    send_dp(8, lambda peer: pfull.at[:, mine], pfull.at[:, mine])

    take(down, HALF, HALF)
    take(up, 0, HALF)
    for owner, h in ((other(down), 0), (other(up), 1), (other(down), 1), (other(up), 0)):
        for i in range(CUTS):
            arrived(owner, h, i)
        take(owner, h * HALF, HALF)

    for i in range(CUTS):
        arrived(far, 0, i)
        ag(far, 0, i, sib)
        arrived(far, 1, i)
        ag(far, 1, i, sib)
    take(far, 0, TOK)
    for h in range(2):
        for i in range(CUTS):
            arrived(other(far), h, i)
    take(other(far), 0, TOK)

    @pl.loop(0, TOK // STEP)
    def _(k):
        r = pl.ds(pl.multiple_of(k * STEP, STEP), STEP)
        res[r, :] = (res[r, :].astype(F32) + proj[r, :] - tch[r, :].astype(F32)).astype(BF16)

    wait_all(x_recv, 8, pfull.at[:, pl.ds(0, FEAT - PIECE)])

    proj[:, 0:128] = dot(abuf[0], pfull[0])

    @pl.loop(1, TP)
    def _(k):
        proj[:, 0:128] += dot(abuf[k], pfull[k])

    @pl.loop(0, TP)
    def _(k):
        pt[k] = pfull[k].T

    ap = fold(proj[:, 0:128]).T
    ap_high = ap.astype(BF16).astype(F32)
    sub = lax.broadcasted_iota(jnp.int32, ap.shape, 0)
    ap_cat = jnp.where(sub < RANK, ap_high, ap - ap_high).astype(BF16)
    right = dot(ap_cat, res[...]) * (1.0 / 32.0)
    gram = jnp.zeros((128, 128), F32)
    for k in range(TP):
        right += dot(pt[k], ev[k * FEAT : (k + 1) * FEAT, :])
        gram += dot(pt[k], pfull[k])
    right = right[0:RANK] + right[RANK:]
    for i in range(8):
        for j in range(5):
            r_send[i * 5 + j] = right[8 * i : 8 * i + 8, 128 * j : 128 * j + 128]
    for j in range(40, TILES):
        r_send[j] = jnp.zeros((8, 128), F32)
    PER = TILES // DP
    r_recv[d] = r_send[pl.ds(d * PER, PER)]
    send_dp(9, lambda peer: r_send.at[pl.ds(peer * PER, PER)], r_recv.at[d])

    def stored(k):
        r = pl.ds(pl.multiple_of(k * FEAT, FEAT), FEAT)
        return pltpu.make_async_copy(ev.at[r], m_hbm.at[r], out_sem.at[k])

    def matrix(k):
        for half in range(2):
            r = pl.ds(pl.multiple_of(k * FEAT + half * 256, 256), 256)
            grad = dot(at[k, half * 256 : half * 256 + 256, :], res[...]) * (1.0 / 32.0)
            ev[r, :] = (grad + ev[r, :].astype(F32)).astype(BF16)
        stored(k).start()

    pl.loop(0, TP // 2)(matrix)

    wait_all(x_recv, 9, r_recv.at[pl.ds(0, DP - 1)])
    total = r_recv[0]
    for k in range(1, DP):
        total += r_recv[k]
    r_full[pl.ds(d * PER, PER)] = total
    send_dp(10, lambda peer: r_full.at[pl.ds(d * PER, PER)], r_full.at[pl.ds(d * PER, PER)])

    linv = inverse_factor(fold(gram[0:RANK] + gram[RANK:]))
    lsplit = split(linv)
    lhigh = linv.astype(BF16).astype(F32)
    back = jnp.concatenate([lhigh, linv - lhigh], axis=0).T.astype(BF16)

    @pl.loop(0, TP)
    def _(k):
        r = pl.ds(pl.multiple_of(k * FEAT, FEAT), FEAT)
        phat_ref[r, :] = split(fold(dot(pfull[k], back)))

    pl.loop(TP // 2, TP)(matrix)

    wait_all(x_recv, 10, r_full.at[pl.ds(0, TILES - PER)])
    summed = jnp.concatenate(
        [jnp.concatenate([r_full[i * 5 + j] for j in range(5)], axis=1) for i in range(8)], axis=0
    )
    rhigh, rlow = split_rows(summed)
    qnext_ref[...] = (dot(lsplit, rhigh) + dot(lsplit, rlow)) * (1.0 / DP)

    for i, like in (
        (0, wq_recv.at[pl.ds(0, TP - 1)]),
        (1, e_recv.at[pl.ds(0, DP - 1)]),
        (2, wq_full.at[pl.ds(0, FEAT - PIECE)]),
        (3, dq_recv.at[pl.ds(0, TP - 1)]),
        (4, dq_full.at[pl.ds(0, TOK - TOKP)]),
        (5, e2_recv.at[pl.ds(0, TP - 1)]),
        (6, pa_recv.at[pl.ds(0, DP - 1)]),
        (7, pfull.at[0, pl.ds(0, (TP - 1) * PIECE)]),
        (8, pfull.at[:, pl.ds(0, FEAT - PIECE)]),
        (9, r_recv.at[pl.ds(0, DP - 1)]),
        (10, r_full.at[pl.ds(0, TILES - PER)]),
    ):
        wait_all(x_send, i, like)
    for copy in sends:
        copy.wait_send()

    @pl.loop(0, TP)
    def _(k):
        stored(k).wait()


def write_kernel(m_ref, phat_ref, qt_ref, out_ref, qout_ref):
    q = qt_ref[...]
    qhigh, qlow = split_rows(q)
    cat = phat_ref[...]
    approx = dot(jnp.concatenate([cat, cat], axis=1), jnp.concatenate([qhigh, qlow], axis=0))
    out_ref[...] = (m_ref[...].astype(F32) - approx).astype(BF16)
    qout_ref[...] = q


def per_device(attn_out, residual_in, teacher, out_weight, error_buf, q_start):
    any_space = pl.BlockSpec(memory_space=pl.ANY)
    vmem = pl.BlockSpec(memory_space=pltpu.VMEM)
    V, S = pltpu.VMEM, pltpu.SemaphoreType.DMA
    n_ag = CUTS * 2 * 7
    m, phat, qt = pl.pallas_call(
        main_kernel,
        name="gather_and_factors",
        out_shape=(
            jax.ShapeDtypeStruct((ROWS, COLS), BF16),
            jax.ShapeDtypeStruct((ROWS, 128), BF16),
            jax.ShapeDtypeStruct((RANK, COLS), F32),
        ),
        in_specs=[any_space] * 5 + [vmem],
        out_specs=(any_space, vmem, vmem),
        scratch_shapes=[
            V((TP, TOK, FEAT), BF16),
            V((TP, FEAT, TOK), BF16),
            V((TP, FEAT, COLS), BF16),
            V((ROWS, COLS), BF16),
            V((TOK, COLS), BF16),
            V((TOK, COLS), BF16),
            V((TOK, COLS), F32),
            V((TP, PIECE, COLS), BF16),
            V((COLS, 128), BF16),
            V((TOK, 128), F32),
            V((TP, PIECE, 128), BF16),
            V((TP, PIECE, 128), BF16),
            V((FEAT, 128), BF16),
            V((TOK, 128), BF16),
            V((TP, TOKP, 128), BF16),
            V((TOK, 128), BF16),
            V((FEAT, 128), BF16),
            V((DP, PIECE, 128), BF16),
            V((TP, FEAT, 128), BF16),
            V((DP, TP, PIECE, 128), BF16),
            V((TP, PIECE, 128), BF16),
            V((TP, PIECE, 128), BF16),
            V((TP, FEAT, 128), BF16),
            V((TP, 128, FEAT), BF16),
            V((TILES, 8, 128), F32),
            V((DP, TILES // DP, 8, 128), F32),
            V((TILES, 8, 128), F32),
            S((6,)),
            S((n_ag,)),
            S((TP, 2, CUTS)),
            S((11,)),
            S((11,)),
            S((TP,)),
        ],
        compiler_params=pltpu.CompilerParams(
            collective_id=0, has_side_effects=True, vmem_limit_bytes=60 * 2**20
        ),
    )(
        attn_out, residual_in, teacher,
        out_weight.reshape(TP, FEAT, COLS),
        error_buf[0], q_start.T,
    )
    block = 512
    error_next, q_next = pl.pallas_call(
        write_kernel,
        name="write_error",
        grid=(ROWS // block,),
        out_shape=(
            jax.ShapeDtypeStruct((ROWS, COLS), BF16),
            jax.ShapeDtypeStruct((RANK, COLS), F32),
        ),
        in_specs=[
            pl.BlockSpec((block, COLS), lambda i: (i, 0)),
            pl.BlockSpec((block, 128), lambda i: (i, 0)),
            pl.BlockSpec((RANK, COLS), lambda i: (0, 0)),
        ],
        out_specs=(
            pl.BlockSpec((block, COLS), lambda i: (i, 0)),
            pl.BlockSpec((RANK, COLS), lambda i: (0, 0)),
        ),
        compiler_params=pltpu.CompilerParams(vmem_limit_bytes=60 * 2**20),
    )(m, phat, qt)
    return error_next[None], q_next.T


def solution(mesh):
    return jax.shard_map(
        per_device,
        mesh=mesh,
        in_specs=(
            P("dp", "tp"),
            P("dp", "tp"),
            P("dp", "tp"),
            P(None, "tp"),
            P("dp", None, "tp"),
            P("tp", None),
        ),
        out_specs=(P("dp", None, "tp"), P("tp", None)),
        check_vma=False,
    )
```

time: 378 us -> 113 us (0.30)
  waiting for transfers between devices: 274 us -> 0 us
  Pallas kernels: 0 us -> 112 us
  matrix products: 56.1 us -> 0 us
  local copies, waits for them, and re-layouts: 19.9 us -> 0 us
  between operations: 13.9 us -> 0.64 us
  other arithmetic: 13 us -> 0 us
    psum x2 -> x0, waiting for transfers between devices: 227 us -> none  [the longest x1 147 us: per_device(): left_sum = lax.psum(left_part, ('dp', 'tp')) / replicas]
    pallas_call x0 -> x2, Pallas kernels: none -> 112 us  [the longest x1 103 us: per_device(): pl.pallas_call(main_kernel, name='gather_and_factors', out_shape=(jax.Sha...]
    dot_general x6 -> x0, matrix products: 53.7 us -> none  [the longest x1 13.4 us: per_device(): lax.dot_general(matrix, basis, (((0,), (0,)), ((), ())), precision=lax.Pr...]
    all_gather x1 -> x0, waiting for transfers between devices: 45.9 us -> none  [per_device(): heads_full = lax.all_gather(attn_out, 'tp', axis=1, tiled=True)]
    unnamed x16 -> x0, local copies, waits for them, and re-layouts: 19.8 us -> none
    another operation x5 -> x0, other arithmetic: 12.1 us -> none  [the longest x3 6.52 us: orthonormal_rows(): lower_factor = jnp.linalg.cholesky(gram_matrix)]
  transfers between devices with their start and end apart: 3 -> 0, of which waited for: 3 -> 0; matrix products, arithmetic and copies ran while one was open for 2% -> 0% of each run, Pallas kernels for 0% -> 0%
where the time goes in v1:
time: 113 us; the launch traced here: 112 us
  Pallas kernels  112 us (99%)
    pallas_call x1, Pallas kernels, per_device(): pl.pallas_call(main_kernel, name='gather_and_factors', out_shape=(jax.Sha...  103 us
    pallas_call x1, Pallas kernels, per_device(): pl.pallas_call(write_kernel, name='write_error', grid=(ROWS // block,), o...  8.65 us

profile of v1, /device:TPU:0, one launch (start us, length us, event | category | flops | bytes accessed | tf_op | source)
XLA Modules:
  0.0 112.2 jit_solution(15220925329111151923)
XLA Ops:
  0.6 103.0 %gather_and_factors.1 = (bf16[4096,640]{1,0:T(8,128)(2,1)}, bf16[4096,128]{1,0:T(8,128)(2,1)}, f32[64,640]{1,0:T(8,128)}) custom-call(bf16[1024,512]{1,0:T(8,128)(2,1)} %a_hbm.1, bf16[1024,640]{1,0:T(8,128)(2,1)} %res_hbm.1, bf16[1024,640]{1,0:T(8,128)(2,1)} %tch_hbm.1, bf16[8,512,640]{2,1,0:T(8,128)(2,1)} %bitcast.5, bf16[4096,640]{1,0:T(8,128)(2,1)} %bitcast.6, ...), custom_call_target="tpu_custom_call" | custom-call | tf_op jit(solution)/shard_map/gather_and_factors/pallas_call | solution.py:415
  103.6 8.7 %write_error.1 = (bf16[4096,640]{1,0:T(8,128)(2,1)}, f32[64,640]{1,0:T(8,128)}) custom-call(bf16[4096,640]{1,0:T(8,128)(2,1)} %get-tuple-element.7.m_ref, bf16[4096,128]{1,0:T(8,128)(2,1)} %get-tuple-element.8.phat_ref, f32[64,640]{1,0:T(8,128)} %get-tuple-element.9.qt_ref), custom_call_target="tpu_custom_call" | custom-call | tf_op jit(solution)/shard_map/write_error/pallas_call | solution.py:469

commit v2 on v1

v2 whole, which is shorter than its diff:
```python
import jax
import jax.numpy as jnp
from jax import lax
from jax.experimental import pallas as pl
from jax.experimental.pallas import tpu as pltpu
from jax.sharding import PartitionSpec as P

MESH = pl.DeviceIdType.MESH
F32, BF16 = jnp.float32, jnp.bfloat16
DP, TP = 16, 8
TOK, FEAT, COLS, RANK = 1024, 512, 640, 64
ROWS = FEAT * TP
PIECE = FEAT // DP
TOKP = TOK // TP
HALF = TOK // 2
CUTS = 2
CUT = HALF // CUTS
TILES = 48


def dot(a, b):
    return jnp.dot(a, b, preferred_element_type=F32)


def fold(x):
    return x + pltpu.roll(x, RANK, 1)


def split(x):
    lane = lax.broadcasted_iota(jnp.int32, x.shape, 1)
    high = x.astype(BF16).astype(F32)
    return jnp.where(lane < RANK, high, x - high).astype(BF16)


def split_rows(x):
    high = x.astype(BF16).astype(F32)
    low = x - high
    return (
        jnp.concatenate([high, high], axis=0).astype(BF16),
        jnp.concatenate([low, low], axis=0).astype(BF16),
    )


def inverse_factor(gram):
    lane = lax.broadcasted_iota(jnp.int32, (8, 128), 1)
    sub = lax.broadcasted_iota(jnp.int32, (8, 128), 0)
    blocks = []
    for b in range(8):
        eye = jnp.where(lane == sub + (RANK + 8 * b), 1.0, 0.0)
        blocks.append(jnp.where(lane < RANK, gram[8 * b : 8 * b + 8, :], eye))
    for k in range(RANK):
        home, at = k // 8, k % 8
        pivot = jnp.broadcast_to(blocks[home][at : at + 1, :], (8, 128))
        scaled = pivot / jnp.broadcast_to(pivot[:, k : k + 1], (8, 128))
        for b in range(home, 8):
            column = jnp.broadcast_to(blocks[b][:, k : k + 1], (8, 128))
            if b == home:
                column = jnp.where(sub > at, column, 0.0)
            blocks[b] = blocks[b] - column * scaled
    out = []
    for b in range(8):
        diagonal = jnp.sum(jnp.where(lane == sub + 8 * b, blocks[b], 0.0), axis=1, keepdims=True)
        rows = jnp.where(lane < RANK, 0.0, blocks[b] * lax.rsqrt(diagonal))
        out.append(fold(rows))
    return jnp.concatenate(out, axis=0)


def main_kernel(
    a_hbm, res_hbm, tch_hbm, w_hbm, e_hbm, qt_ref,
    m_hbm, p_hbm, coef_ref, qnext_ref,
    abuf, at, wv, ev, res, tch, proj, wblk, qcat, xq,
    wq_send, wq_recv, wq_full, dq_send, dq_recv, dq_full,
    pa_send, pa_recv, eq_send, e0_recv, e1_send, e_recv, e2_send, e2_recv, pfull, pt,
    r_send, r_recv, r_full,
    load_sem, ag_send, ag_recv, x_send, x_recv, p_recv, out_sem,
):
    d, t = lax.axis_index("dp"), lax.axis_index("tp")
    y, c = t // 2, lax.rem(t, 2)
    sib = y * 2 + 1 - c
    up = lax.rem(y + 1, 4) * 2 + c
    down = lax.rem(y + 3, 4) * 2 + c
    far = lax.rem(y + 2, 4) * 2 + c
    odown, oup, ofar = (lax.rem(y + k, 4) * 2 + 1 - c for k in (3, 1, 2))

    mine = pl.ds(pl.multiple_of(d * PIECE, PIECE), PIECE)
    load_blk = pltpu.make_async_copy(w_hbm.at[:, mine], wblk, load_sem.at[0])
    load_a = pltpu.make_async_copy(a_hbm, abuf.at[t], load_sem.at[1])
    load_e = pltpu.make_async_copy(e_hbm, ev, load_sem.at[2])
    load_res = pltpu.make_async_copy(res_hbm, res, load_sem.at[3])
    load_tch = pltpu.make_async_copy(tch_hbm, tch, load_sem.at[4])
    load_w = pltpu.make_async_copy(w_hbm, wv, load_sem.at[5])
    for load in (load_blk, load_e, load_a, load_res, load_tch, load_w):
        load.start()

    barrier = pltpu.get_barrier_semaphore()

    @pl.loop(1, TP)
    def _(k):
        pl.semaphore_signal(barrier, inc=1, device_id={"tp": lax.rem(t + k, TP)}, device_id_type=MESH)

    @pl.loop(1, DP)
    def _(k):
        pl.semaphore_signal(barrier, inc=1, device_id={"dp": lax.rem(d + k, DP)}, device_id_type=MESH)

    q = qt_ref[...]
    high = q.astype(BF16).astype(F32)
    qcat[...] = jnp.concatenate([high, q - high], axis=0).T.astype(BF16)

    load_blk.wait()
    part = dot(wblk[...].reshape(TP * PIECE, COLS), qcat[...])
    wq_send[...] = split(fold(part)).reshape(TP, PIECE, 128)
    wq_recv[t] = wq_send[t]

    pl.semaphore_wait(barrier, TP - 1 + DP - 1)

    started = {}

    def remote(i, src, dst, peer, recv=None):
        pltpu.make_async_remote_copy(
            src, dst, x_send.at[i], x_recv.at[i] if recv is None else recv,
            device_id=peer, device_id_type=MESH,
        ).start()

    def send_tp(i, src, dst, like):
        started[i] = like

        @pl.loop(1, TP)
        def _(k):
            peer = lax.rem(t + k, TP)
            remote(i, src(peer), dst, {"tp": peer})

    def send_y(i, src, dst, like):
        started[i] = like

        @pl.loop(1, 4)
        def _(k):
            peer = lax.rem(y + k, 4)
            remote(i, src(peer), dst, {"tp": peer * 2 + c})

    def send_dp(i, src, dst, like, recv=None):
        started[i] = like

        @pl.loop(1, DP)
        def _(k):
            peer = lax.rem(d + k, DP)
            remote(i, src(peer), dst, {"dp": peer}, recv)

    def wait_all(i):
        pltpu.make_async_copy(started[i], started[i], x_recv.at[i]).wait()

    sends = []

    def rows(h, i):
        return pl.ds(h * HALF + i * CUT, CUT)

    def ag(owner, h, i, dest, src=None):
        r = rows(h, i)
        copy = pltpu.make_async_remote_copy(
            abuf.at[owner, r] if src is None else src.at[r], abuf.at[owner, r],
            ag_send.at[len(sends)], ag_recv.at[owner, h, i],
            device_id={"tp": dest}, device_id_type=MESH,
        )
        copy.start()
        sends.append(copy)

    def arrived(owner, h, i):
        r = rows(h, i)
        pltpu.make_async_copy(abuf.at[owner, r], abuf.at[owner, r], ag_recv.at[owner, h, i]).wait()

    send_tp(0, lambda peer: wq_send.at[peer], wq_recv.at[t], wq_recv.at[pl.ds(0, TP - 1)])
    for hh in range(2):
        for i in range(CUTS):
            ag(t, hh, i, up, a_hbm)
            ag(t, 1 - hh, i, down, a_hbm)

    load_e.wait()

    @pl.loop(0, TP)
    def _(k):
        block = ev[pl.ds(pl.multiple_of(k * FEAT, FEAT), FEAT), :]
        eq_send[k // 2, lax.rem(k, 2)] = split(fold(dot(block, qcat[...])))

    started[1] = e0_recv
    remote(1, eq_send.at[:, 1 - c], e0_recv, {"tp": sib})
    for h in range(2):
        for i in range(CUTS):
            ag(t, h, i, sib, a_hbm)

    def piece(peer):
        return pl.ds(pl.multiple_of(peer * PIECE, PIECE), PIECE)

    wait_all(0)
    total = wq_recv[0].astype(F32)
    for k in range(1, TP):
        total += wq_recv[k].astype(F32)
    wq_full[mine, :] = split(fold(total))
    send_dp(2, lambda peer: wq_full.at[mine], wq_full.at[mine], wq_full.at[pl.ds(0, FEAT - PIECE)])

    wait_all(1)

    @pl.loop(0, 4)
    def _(k):
        e1_send[k] = split(fold(eq_send[k, c].astype(F32) + e0_recv[k].astype(F32)))

    e_recv[d] = e1_send[:, mine, :]
    send_dp(5, lambda peer: e1_send.at[:, piece(peer)], e_recv.at[d], e_recv.at[pl.ds(0, DP - 1)])

    load_res.wait()
    load_tch.wait()
    STEP = 512

    @pl.loop(0, TOK // STEP)
    def _(k):
        r = pl.ds(pl.multiple_of(k * STEP, STEP), STEP)
        xq[r, :] = dot(res[r, :], qcat[...]) - dot(tch[r, :], qcat[...])

    load_a.wait()
    load_w.wait()

    def take(owner, lo, n, first=False):
        @pl.loop(0, n // STEP)
        def _(k):
            r = pl.ds(pl.multiple_of(lo + k * STEP, STEP), STEP)
            block = abuf[owner, r, :]
            at[owner, :, r] = block.T
            term = dot(block, wv[owner])
            if first:
                proj[r, :] = term
            else:
                proj[r, :] += term

    take(t, 0, TOK, first=True)

    wait_all(2)

    @pl.loop(0, TOK // STEP)
    def _(k):
        r = pl.ds(pl.multiple_of(k * STEP, STEP), STEP)
        part = xq[r, :] + dot(abuf[t, r, :], wq_full[...])
        dq_send[r, :] = split(fold(part))

    def tokens(peer):
        return pl.ds(pl.multiple_of(peer * TOKP, TOKP), TOKP)

    dq_recv[t] = dq_send[tokens(t), :]
    send_tp(3, lambda peer: dq_send.at[tokens(peer)], dq_recv.at[t], dq_recv.at[pl.ds(0, TP - 1)])

    for h in range(2):
        for i in range(CUTS):
            arrived(sib, h, i)
    take(sib, 0, TOK)

    wait_all(3)
    total = dq_recv[0].astype(F32)
    for k in range(1, TP):
        total += dq_recv[k].astype(F32)
    dq_full[tokens(t), :] = split(fold(total))
    send_tp(4, lambda peer: dq_full.at[tokens(t)], dq_full.at[tokens(t)], dq_full.at[pl.ds(0, TOK - TOKP)])

    for i in range(CUTS):
        arrived(down, 0, i)
        ag(down, 0, i, up)
        ag(down, 0, i, sib)
        arrived(up, 1, i)
        ag(up, 1, i, down)
        ag(up, 1, i, sib)

    wait_all(4)
    part = dot(at[t], dq_full[...]) * (1.0 / 32.0)
    pa_send[...] = split(fold(part))
    pa_recv[d] = pa_send[mine, :]
    send_dp(7, lambda peer: pa_send.at[piece(peer)], pa_recv.at[d], pa_recv.at[pl.ds(0, DP - 1)])

    wait_all(5)

    @pl.loop(0, 4)
    def _(k):
        total = e_recv[0, k].astype(F32)
        for j in range(1, DP):
            total += e_recv[j, k].astype(F32)
        e2_send[k] = split(fold(total))

    e2_recv[y] = e2_send[y]
    send_y(6, lambda peer: e2_send.at[peer], e2_recv.at[y], e2_recv.at[pl.ds(0, 3)])

    take(down, 0, HALF)
    take(up, HALF, HALF)

    wait_all(6)
    wait_all(7)
    total = e2_recv[0].astype(F32)
    for k in range(1, 4):
        total += e2_recv[k].astype(F32)
    for k in range(DP):
        total += pa_recv[k].astype(F32)
    pfull[y, c, mine, :] = split(fold(total) * (1.0 / DP))
    send_y(8, lambda peer: pfull.at[y, c, mine], pfull.at[y, c, mine], pfull.at[0, 0, pl.ds(0, 3 * PIECE)])

    for i in range(CUTS):
        arrived(down, 1, i)
        ag(down, 1, i, sib)
        arrived(up, 0, i)
        ag(up, 0, i, sib)

    wait_all(8)
    send_dp(9, lambda peer: pfull.at[:, c, mine], pfull.at[:, c, mine],
            pfull.at[:, 0, pl.ds(0, FEAT - PIECE)], p_recv.at[d])
    started[10] = pfull.at[:, 1 - c]
    remote(10, pfull.at[:, c, mine], pfull.at[:, c, mine], {"tp": sib})

    take(down, HALF, HALF)
    take(up, 0, HALF)
    for owner, h in ((odown, 0), (oup, 1), (odown, 1), (oup, 0)):
        for i in range(CUTS):
            arrived(owner, h, i)
        take(owner, h * HALF, HALF)

    @pl.loop(1, DP)
    def _(k):
        source = lax.rem(d + DP - k, DP)
        block = pfull.at[:, c, piece(source)]
        pltpu.make_async_copy(block, block, p_recv.at[source]).wait()
        remote(10, block, block, {"tp": sib})

    for i in range(CUTS):
        arrived(far, 0, i)
        ag(far, 0, i, sib)
        arrived(far, 1, i)
        ag(far, 1, i, sib)
    take(far, 0, TOK)

    wait_all(10)
    copy_p = pltpu.make_async_copy(pfull, p_hbm, out_sem.at[TP])
    copy_p.start()
    right = jnp.zeros((128, COLS), F32)
    gram = jnp.zeros((128, 128), F32)
    for k in range(TP):
        pt[k] = pfull[k // 2, k % 2].T
        right += dot(pt[k], ev[k * FEAT : (k + 1) * FEAT, :])
        gram += dot(pt[k], pfull[k // 2, k % 2])
    linv = inverse_factor(fold(gram[0:RANK] + gram[RANK:]))

    for h in range(2):
        for i in range(CUTS):
            arrived(ofar, h, i)
    take(ofar, 0, TOK)

    @pl.loop(0, TOK // STEP)
    def _(k):
        r = pl.ds(pl.multiple_of(k * STEP, STEP), STEP)
        res[r, :] = (res[r, :].astype(F32) + proj[r, :] - tch[r, :].astype(F32)).astype(BF16)

    ap = dot(pt[0], at[0])
    for k in range(1, TP):
        ap += dot(pt[k], at[k])
    ap = ap[0:RANK] + ap[RANK:]
    ap_high = ap.astype(BF16).astype(F32)
    ap_cat = jnp.concatenate([ap_high, ap - ap_high], axis=0).astype(BF16)
    right += dot(ap_cat, res[...]) * (1.0 / 32.0)
    right = right[0:RANK] + right[RANK:]
    for i in range(8):
        for j in range(5):
            r_send[i * 5 + j] = right[8 * i : 8 * i + 8, 128 * j : 128 * j + 128]
    for j in range(40, TILES):
        r_send[j] = jnp.zeros((8, 128), F32)
    PER = TILES // DP
    r_recv[d] = r_send[pl.ds(d * PER, PER)]
    send_dp(11, lambda peer: r_send.at[pl.ds(peer * PER, PER)], r_recv.at[d], r_recv.at[pl.ds(0, DP - 1)])

    def stored(k):
        r = pl.ds(pl.multiple_of(k * 2 * FEAT, 2 * FEAT), 2 * FEAT)
        return pltpu.make_async_copy(ev.at[r], m_hbm.at[r], out_sem.at[k])

    def matrix(k):
        r = pl.ds(pl.multiple_of(k * 2 * FEAT, 2 * FEAT), 2 * FEAT)
        grad = dot(at[pl.ds(2 * k, 2)].reshape(2 * FEAT, TOK), res[...]) * (1.0 / 32.0)
        ev[r, :] = (grad + ev[r, :].astype(F32)).astype(BF16)
        stored(k).start()

    pl.loop(0, 2)(matrix)

    wait_all(11)
    total = r_recv[0]
    for k in range(1, DP):
        total += r_recv[k]
    r_full[pl.ds(d * PER, PER)] = total
    send_dp(12, lambda peer: r_full.at[pl.ds(d * PER, PER)], r_full.at[pl.ds(d * PER, PER)],
            r_full.at[pl.ds(0, TILES - PER)])

    pl.loop(2, 4)(matrix)
    lhigh = linv.astype(BF16).astype(F32)
    lcat = split(linv)
    lhigh2 = lhigh.T
    ltcat = jnp.concatenate([lhigh2[0:RANK], (linv - lhigh).T[0:RANK]], axis=1).astype(BF16)

    wait_all(12)
    summed = jnp.concatenate(
        [jnp.concatenate([r_full[i * 5 + j] for j in range(5)], axis=1) for i in range(8)], axis=0
    )
    rhigh, rlow = split_rows(summed)
    qt = (dot(lcat, rhigh) + dot(lcat, rlow)) * (1.0 / DP)
    qnext_ref[...] = qt
    rhigh, rlow = split_rows(qt)
    coef = dot(ltcat, rhigh) + dot(ltcat, rlow)
    chigh, clow = split_rows(coef)
    coef_ref[...] = jnp.concatenate([chigh, clow], axis=0)

    for i, like in started.items():
        pltpu.make_async_copy(like, like, x_send.at[i]).wait()
    for copy in sends:
        copy.wait_send()
    copy_p.wait()

    @pl.loop(0, 4)
    def _(k):
        stored(k).wait()


CHUNKS = 8
CHUNK = ROWS // CHUNKS


def write_kernel(m_hbm, p_hbm, coef_ref, qt_ref, out_hbm, qout_ref, m, p, out, m_sem, p_sem, out_sem):
    def load(k):
        r = pl.ds(pl.multiple_of(k * CHUNK, CHUNK), CHUNK)
        return (
            pltpu.make_async_copy(m_hbm.at[r], m.at[r], m_sem.at[k]),
            pltpu.make_async_copy(p_hbm.at[k // 2, lax.rem(k, 2)], p.at[r], p_sem.at[k]),
        )

    def store(k):
        r = pl.ds(pl.multiple_of(k * CHUNK, CHUNK), CHUNK)
        return pltpu.make_async_copy(out.at[r], out_hbm.at[r], out_sem.at[k])

    @pl.loop(0, CHUNKS)
    def _(k):
        for copy in load(k):
            copy.start()

    qout_ref[...] = qt_ref[...]

    @pl.loop(0, CHUNKS)
    def _(k):
        for copy in load(k):
            copy.wait()
        r = pl.ds(pl.multiple_of(k * CHUNK, CHUNK), CHUNK)
        cat = p[r, :]
        approx = dot(jnp.concatenate([cat, cat], axis=1), coef_ref[...])
        out[r, :] = (m[r, :].astype(F32) - approx).astype(BF16)
        store(k).start()

    @pl.loop(0, CHUNKS)
    def _(k):
        store(k).wait()


def per_device(attn_out, residual_in, teacher, out_weight, error_buf, q_start):
    any_space = pl.BlockSpec(memory_space=pl.ANY)
    vmem = pl.BlockSpec(memory_space=pltpu.VMEM)
    V, S = pltpu.VMEM, pltpu.SemaphoreType.DMA
    n_ag = CUTS * 2 * 7
    m, p, coef, qt = pl.pallas_call(
        main_kernel,
        name="gather_and_factors",
        out_shape=(
            jax.ShapeDtypeStruct((ROWS, COLS), BF16),
            jax.ShapeDtypeStruct((4, 2, FEAT, 128), BF16),
            jax.ShapeDtypeStruct((256, COLS), BF16),
            jax.ShapeDtypeStruct((RANK, COLS), F32),
        ),
        in_specs=[any_space] * 5 + [vmem],
        out_specs=(any_space, any_space, vmem, vmem),
        scratch_shapes=[
            V((TP, TOK, FEAT), BF16),
            V((TP, FEAT, TOK), BF16),
            V((TP, FEAT, COLS), BF16),
            V((ROWS, COLS), BF16),
            V((TOK, COLS), BF16),
            V((TOK, COLS), BF16),
            V((TOK, COLS), F32),
            V((TP, PIECE, COLS), BF16),
            V((COLS, 128), BF16),
            V((TOK, 128), F32),
            V((TP, PIECE, 128), BF16),
            V((TP, PIECE, 128), BF16),
            V((FEAT, 128), BF16),
            V((TOK, 128), BF16),
            V((TP, TOKP, 128), BF16),
            V((TOK, 128), BF16),
            V((FEAT, 128), BF16),
            V((DP, PIECE, 128), BF16),
            V((4, 2, FEAT, 128), BF16),
            V((4, FEAT, 128), BF16),
            V((4, FEAT, 128), BF16),
            V((DP, 4, PIECE, 128), BF16),
            V((4, PIECE, 128), BF16),
            V((4, PIECE, 128), BF16),
            V((4, 2, FEAT, 128), BF16),
            V((TP, 128, FEAT), BF16),
            V((TILES, 8, 128), F32),
            V((DP, TILES // DP, 8, 128), F32),
            V((TILES, 8, 128), F32),
            S((6,)),
            S((n_ag,)),
            S((TP, 2, CUTS)),
            S((13,)),
            S((13,)),
            S((DP,)),
            S((TP + 1,)),
        ],
        compiler_params=pltpu.CompilerParams(
            collective_id=0, has_side_effects=True, vmem_limit_bytes=60 * 2**20
        ),
    )(
        attn_out, residual_in, teacher,
        out_weight.reshape(TP, FEAT, COLS),
        error_buf[0], q_start.T,
    )
    error_next, q_next = pl.pallas_call(
        write_kernel,
        name="write_error",
        out_shape=(
            jax.ShapeDtypeStruct((ROWS, COLS), BF16),
            jax.ShapeDtypeStruct((RANK, COLS), F32),
        ),
        in_specs=[any_space, any_space, vmem, vmem],
        out_specs=(any_space, vmem),
        scratch_shapes=[
            V((ROWS, COLS), BF16),
            V((ROWS, 128), BF16),
            V((ROWS, COLS), BF16),
            S((CHUNKS,)),
            S((CHUNKS,)),
            S((CHUNKS,)),
        ],
        compiler_params=pltpu.CompilerParams(vmem_limit_bytes=60 * 2**20),
    )(m, p, coef, qt)
    return error_next[None], q_next.T


def solution(mesh):
    return jax.shard_map(
        per_device,
        mesh=mesh,
        in_specs=(
            P("dp", "tp"),
            P("dp", "tp"),
            P("dp", "tp"),
            P(None, "tp"),
            P("dp", None, "tp"),
            P("tp", None),
        ),
        out_specs=(P("dp", None, "tp"), P("tp", None)),
        check_vma=False,
    )
```

time: 113 us -> 99.9 us (0.88)
  Pallas kernels: 112 us -> 99 us
    pallas_call x1, Pallas kernels: 103 us -> 92.1 us  [per_device(): pl.pallas_call(main_kernel, name='gather_and_factors', out_shape=(jax.Sha...]
    pallas_call x1, Pallas kernels: 8.65 us -> 6.83 us  [per_device(): pl.pallas_call(write_kernel, name='write_error', out_shape=(jax.ShapeDtyp...]
where the time goes in v2:
time: 99.9 us; the launch traced here: 99.8 us
  Pallas kernels  99 us (99%)
    pallas_call x1, Pallas kernels, per_device(): pl.pallas_call(main_kernel, name='gather_and_factors', out_shape=(jax.Sha...  92.1 us
    pallas_call x1, Pallas kernels, per_device(): pl.pallas_call(write_kernel, name='write_error', out_shape=(jax.ShapeDtyp...  6.83 us

profile of v2, /device:TPU:0, one launch (start us, length us, event | category | flops | bytes accessed | tf_op | source)
XLA Modules:
  0.0 99.8 jit_solution(11110518133568834905)
XLA Ops:
  0.6 92.1 %gather_and_factors.1 = (bf16[4096,640]{1,0:T(8,128)(2,1)}, bf16[4,2,512,128]{3,2,1,0:T(8,128)(2,1)}, bf16[256,640]{1,0:T(8,128)(2,1)}, f32[64,640]{1,0:T(8,128)}) custom-call(bf16[1024,512]{1,0:T(8,128)(2,1)} %a_hbm.1, bf16[1024,640]{1,0:T(8,128)(2,1)} %res_hbm.1, bf16[1024,640]{1,0:T(8,128)(2,1)} %tch_hbm.1, bf16[8,512,640]{2,1,0:T(8,128)(2,1)} %bitcast.5, ...), custom_call_target="tpu_custom_call" | custom-call | tf_op jit(solution)/shard_map/gather_and_factors/pallas_call | solution.py:462
  92.8 6.8 %write_error.1 = (bf16[4096,640]{1,0:T(8,128)(2,1)}, f32[64,640]{1,0:T(8,128)}) custom-call(bf16[4096,640]{1,0:T(8,128)(2,1)} %get-tuple-element.8.m_hbm, bf16[4,2,512,128]{3,2,1,0:T(8,128)(2,1)} %get-tuple-element.9.p_hbm, bf16[256,640]{1,0:T(8,128)(2,1)} %get-tuple-element.10.coef_ref, f32[64,640]{1,0:T(8,128)} %get-tuple-element.11.qt_ref), custom_call_target="tpu_custom_call" | custom-call | tf_op jit(solution)/shard_map/write_error/pallas_call | solution.py:519

commit v3 on v2

--- a/solution.py
+++ b/solution.py
@@ -13,9 +13,10 @@
 PIECE = FEAT // DP
 TOKP = TOK // TP
 HALF = TOK // 2
-CUTS = 2
+CUTS = 4
 CUT = HALF // CUTS
 TILES = 48
+W2, W3 = 1, 1
 
 
 def dot(a, b):
@@ -89,7 +90,7 @@
     load_res = pltpu.make_async_copy(res_hbm, res, load_sem.at[3])
     load_tch = pltpu.make_async_copy(tch_hbm, tch, load_sem.at[4])
     load_w = pltpu.make_async_copy(w_hbm, wv, load_sem.at[5])
-    for load in (load_blk, load_e, load_a, load_res, load_tch, load_w):
+    for load in (load_blk, load_res, load_tch, load_e, load_a, load_w):
         load.start()
 
     barrier = pltpu.get_barrier_semaphore()
@@ -110,6 +111,15 @@
     part = dot(wblk[...].reshape(TP * PIECE, COLS), qcat[...])
     wq_send[...] = split(fold(part)).reshape(TP, PIECE, 128)
     wq_recv[t] = wq_send[t]
+
+    load_res.wait()
+    load_tch.wait()
+    STEP = 512
+
+    @pl.loop(0, TOK // STEP)
+    def _(k):
+        r = pl.ds(pl.multiple_of(k * STEP, STEP), STEP)
+        xq[r, :] = dot(res[r, :], qcat[...]) - dot(tch[r, :], qcat[...])
 
     pl.semaphore_wait(barrier, TP - 1 + DP - 1)
 
@@ -150,11 +160,11 @@
 
     sends = []
 
-    def rows(h, i):
-        return pl.ds(h * HALF + i * CUT, CUT)
-
-    def ag(owner, h, i, dest, src=None):
-        r = rows(h, i)
+    def rows(h, i, n=1):
+        return pl.ds(h * HALF + i * CUT, n * CUT)
+
+    def ag(owner, h, i, dest, src=None, n=1):
+        r = rows(h, i, n)
         copy = pltpu.make_async_remote_copy(
             abuf.at[owner, r] if src is None else src.at[r], abuf.at[owner, r],
             ag_send.at[len(sends)], ag_recv.at[owner, h, i],
@@ -163,15 +173,22 @@
         copy.start()
         sends.append(copy)
 
-    def arrived(owner, h, i):
-        r = rows(h, i)
+    def arrived(owner, h, i, n=1):
+        r = rows(h, i, n)
         pltpu.make_async_copy(abuf.at[owner, r], abuf.at[owner, r], ag_recv.at[owner, h, i]).wait()
 
-    send_tp(0, lambda peer: wq_send.at[peer], wq_recv.at[t], wq_recv.at[pl.ds(0, TP - 1)])
-    for hh in range(2):
-        for i in range(CUTS):
+    def own(hh, pieces):
+        for i in pieces:
             ag(t, hh, i, up, a_hbm)
             ag(t, 1 - hh, i, down, a_hbm)
+
+    def pass_on(pieces):
+        for i in pieces:
+            ag(down, 0, i, up)
+            ag(up, 1, i, down)
+
+    send_tp(0, lambda peer: wq_send.at[peer], wq_recv.at[t], wq_recv.at[pl.ds(0, TP - 1)])
+    own(0, range(CUTS))
 
     load_e.wait()
 
@@ -183,8 +200,7 @@
     started[1] = e0_recv
     remote(1, eq_send.at[:, 1 - c], e0_recv, {"tp": sib})
     for h in range(2):
-        for i in range(CUTS):
-            ag(t, h, i, sib, a_hbm)
+        ag(t, h, 0, sib, a_hbm, CUTS)
 
     def piece(peer):
         return pl.ds(pl.multiple_of(peer * PIECE, PIECE), PIECE)
@@ -204,15 +220,6 @@
 
     e_recv[d] = e1_send[:, mine, :]
     send_dp(5, lambda peer: e1_send.at[:, piece(peer)], e_recv.at[d], e_recv.at[pl.ds(0, DP - 1)])
-
-    load_res.wait()
-    load_tch.wait()
-    STEP = 512
-
-    @pl.loop(0, TOK // STEP)
-    def _(k):
-        r = pl.ds(pl.multiple_of(k * STEP, STEP), STEP)
-        xq[r, :] = dot(res[r, :], qcat[...]) - dot(tch[r, :], qcat[...])
 
     load_a.wait()
     load_w.wait()
@@ -245,10 +252,26 @@
     dq_recv[t] = dq_send[tokens(t), :]
     send_tp(3, lambda peer: dq_send.at[tokens(peer)], dq_recv.at[t], dq_recv.at[pl.ds(0, TP - 1)])
 
+    own(1, range(0, W2))
     for h in range(2):
+        arrived(sib, h, 0, CUTS)
+    take(sib, 0, TOK)
+    for owner, h in ((down, 0), (up, 1)):
         for i in range(CUTS):
-            arrived(sib, h, i)
-    take(sib, 0, TOK)
+            arrived(owner, h, i)
+        ag(owner, h, 0, sib, None, CUTS)
+        take(owner, h * HALF, HALF)
+
+    wait_all(5)
+
+    @pl.loop(0, 4)
+    def _(k):
+        total = e_recv[0, k].astype(F32)
+        for j in range(1, DP):
+            total += e_recv[j, k].astype(F32)
+        e2_send[k] = split(fold(total))
+
+    e2_recv[y] = e2_send[y]
 
     wait_all(3)
     total = dq_recv[0].astype(F32)
@@ -257,34 +280,18 @@
     dq_full[tokens(t), :] = split(fold(total))
     send_tp(4, lambda peer: dq_full.at[tokens(t)], dq_full.at[tokens(t)], dq_full.at[pl.ds(0, TOK - TOKP)])
 
-    for i in range(CUTS):
-        arrived(down, 0, i)
-        ag(down, 0, i, up)
-        ag(down, 0, i, sib)
-        arrived(up, 1, i)
-        ag(up, 1, i, down)
-        ag(up, 1, i, sib)
+    send_y(6, lambda peer: e2_send.at[peer], e2_recv.at[y], e2_recv.at[pl.ds(0, 3)])
+    own(1, range(W2, CUTS))
+    pass_on(range(0, W3))
+    for owner, h in ((odown, 0), (oup, 1)):
+        arrived(owner, h, 0, CUTS)
+        take(owner, h * HALF, HALF)
 
     wait_all(4)
     part = dot(at[t], dq_full[...]) * (1.0 / 32.0)
     pa_send[...] = split(fold(part))
     pa_recv[d] = pa_send[mine, :]
     send_dp(7, lambda peer: pa_send.at[piece(peer)], pa_recv.at[d], pa_recv.at[pl.ds(0, DP - 1)])
-
-    wait_all(5)
-
-    @pl.loop(0, 4)
-    def _(k):
-        total = e_recv[0, k].astype(F32)
-        for j in range(1, DP):
-            total += e_recv[j, k].astype(F32)
-        e2_send[k] = split(fold(total))
-
-    e2_recv[y] = e2_send[y]
-    send_y(6, lambda peer: e2_send.at[peer], e2_recv.at[y], e2_recv.at[pl.ds(0, 3)])
-
-    take(down, 0, HALF)
-    take(up, HALF, HALF)
 
     wait_all(6)
     wait_all(7)
@@ -296,11 +303,12 @@
     pfull[y, c, mine, :] = split(fold(total) * (1.0 / DP))
     send_y(8, lambda peer: pfull.at[y, c, mine], pfull.at[y, c, mine], pfull.at[0, 0, pl.ds(0, 3 * PIECE)])
 
-    for i in range(CUTS):
-        arrived(down, 1, i)
-        ag(down, 1, i, sib)
-        arrived(up, 0, i)
-        ag(up, 0, i, sib)
+    pass_on(range(W3, CUTS))
+    for owner, h in ((down, 1), (up, 0)):
+        for i in range(CUTS):
+            arrived(owner, h, i)
+        ag(owner, h, 0, sib, None, CUTS)
+        take(owner, h * HALF, HALF)
 
     wait_all(8)
     send_dp(9, lambda peer: pfull.at[:, c, mine], pfull.at[:, c, mine],
@@ -308,11 +316,8 @@
     started[10] = pfull.at[:, 1 - c]
     remote(10, pfull.at[:, c, mine], pfull.at[:, c, mine], {"tp": sib})
 
-    take(down, HALF, HALF)
-    take(up, 0, HALF)
-    for owner, h in ((odown, 0), (oup, 1), (odown, 1), (oup, 0)):
-        for i in range(CUTS):
-            arrived(owner, h, i)
+    for owner, h in ((odown, 1), (oup, 0)):
+        arrived(owner, h, 0, CUTS)
         take(owner, h * HALF, HALF)
 
     @pl.loop(1, DP)
@@ -322,11 +327,11 @@
         pltpu.make_async_copy(block, block, p_recv.at[source]).wait()
         remote(10, block, block, {"tp": sib})
 
-    for i in range(CUTS):
-        arrived(far, 0, i)
-        ag(far, 0, i, sib)
-        arrived(far, 1, i)
-        ag(far, 1, i, sib)
+    for i in range(0, CUTS, 2):
+        for h in range(2):
+            arrived(far, h, i)
+            arrived(far, h, i + 1)
+            ag(far, h, i, sib, None, 2)
     take(far, 0, TOK)
 
     wait_all(10)
@@ -340,9 +345,9 @@
         gram += dot(pt[k], pfull[k // 2, k % 2])
     linv = inverse_factor(fold(gram[0:RANK] + gram[RANK:]))
 
-    for h in range(2):
-        for i in range(CUTS):
-            arrived(ofar, h, i)
+    for i in range(0, CUTS, 2):
+        for h in range(2):
+            arrived(ofar, h, i, 2)
     take(ofar, 0, TOK)
 
     @pl.loop(0, TOK // STEP)
@@ -458,7 +463,7 @@
     any_space = pl.BlockSpec(memory_space=pl.ANY)
     vmem = pl.BlockSpec(memory_space=pltpu.VMEM)
     V, S = pltpu.VMEM, pltpu.SemaphoreType.DMA
-    n_ag = CUTS * 2 * 7
+    n_ag = CUTS * 2 * 3 + 2 * 5 + 2
     m, p, coef, qt = pl.pallas_call(
         main_kernel,
         name="gather_and_factors",

time: 99.9 us -> 88.2 us (0.88)
  Pallas kernels: 99 us -> 87.3 us
    pallas_call x1, Pallas kernels: 92.1 us -> 80.5 us  [per_device(): pl.pallas_call(main_kernel, name='gather_and_factors', out_shape=(jax.Sha...]
where the time goes in v3:
time: 88.2 us; the launch traced here: 88.1 us
  Pallas kernels  87.3 us (99%)
    pallas_call x1, Pallas kernels, per_device(): pl.pallas_call(main_kernel, name='gather_and_factors', out_shape=(jax.Sha...  80.5 us
    pallas_call x1, Pallas kernels, per_device(): pl.pallas_call(write_kernel, name='write_error', out_shape=(jax.ShapeDtyp...  6.83 us

profile of v3, /device:TPU:0, one launch (start us, length us, event | category | flops | bytes accessed | tf_op | source)
XLA Modules:
  0.0 88.1 jit_solution(2480990479865943844)
XLA Ops:
  0.6 80.5 %gather_and_factors.1 = (bf16[4096,640]{1,0:T(8,128)(2,1)}, bf16[4,2,512,128]{3,2,1,0:T(8,128)(2,1)}, bf16[256,640]{1,0:T(8,128)(2,1)}, f32[64,640]{1,0:T(8,128)}) custom-call(bf16[1024,512]{1,0:T(8,128)(2,1)} %a_hbm.1, bf16[1024,640]{1,0:T(8,128)(2,1)} %res_hbm.1, bf16[1024,640]{1,0:T(8,128)(2,1)} %tch_hbm.1, bf16[8,512,640]{2,1,0:T(8,128)(2,1)} %bitcast.5, ...), custom_call_target="tpu_custom_call" | custom-call | tf_op jit(solution)/shard_map/gather_and_factors/pallas_call | solution.py:467
  81.1 6.8 %write_error.1 = (bf16[4096,640]{1,0:T(8,128)(2,1)}, f32[64,640]{1,0:T(8,128)}) custom-call(bf16[4096,640]{1,0:T(8,128)(2,1)} %get-tuple-element.8.m_hbm, bf16[4,2,512,128]{3,2,1,0:T(8,128)(2,1)} %get-tuple-element.9.p_hbm, bf16[256,640]{1,0:T(8,128)(2,1)} %get-tuple-element.10.coef_ref, f32[64,640]{1,0:T(8,128)} %get-tuple-element.11.qt_ref), custom_call_target="tpu_custom_call" | custom-call | tf_op jit(solution)/shard_map/write_error/pallas_call | solution.py:524

commit v4 on v3

--- a/solution.py
+++ b/solution.py
@@ -14,6 +14,7 @@
 TOKP = TOK // TP
 HALF = TOK // 2
 CUTS = 4
+GROUP = 4
 CUT = HALF // CUTS
 TILES = 48
 W2, W3 = 1, 1
@@ -49,15 +50,30 @@
     for b in range(8):
         eye = jnp.where(lane == sub + (RANK + 8 * b), 1.0, 0.0)
         blocks.append(jnp.where(lane < RANK, gram[8 * b : 8 * b + 8, :], eye))
-    for k in range(RANK):
+    for k in range(0, RANK, GROUP):
         home, at = k // 8, k % 8
-        pivot = jnp.broadcast_to(blocks[home][at : at + 1, :], (8, 128))
-        scaled = pivot / jnp.broadcast_to(pivot[:, k : k + 1], (8, 128))
-        for b in range(home, 8):
-            column = jnp.broadcast_to(blocks[b][:, k : k + 1], (8, 128))
-            if b == home:
-                column = jnp.where(sub > at, column, 0.0)
-            blocks[b] = blocks[b] - column * scaled
+        span = range(GROUP)
+        row = [jnp.broadcast_to(blocks[home][at + i : at + i + 1, :], (8, 128)) for i in span]
+        small = [[jnp.broadcast_to(row[i][:, k + j : k + j + 1], (8, 128)) for j in span] for i in span]
+        column = {
+            b: [jnp.broadcast_to(blocks[b][:, k + j : k + j + 1], (8, 128)) for j in span] for b in range(home, 8)
+        }
+        for i in span:
+            inverse = 1.0 / small[i][i]
+            for j in range(i + 1, GROUP):
+                factor = small[i][j] * inverse
+                row[j] = row[j] - factor * row[i]
+                for l in range(i + 1, GROUP):
+                    small[j][l] = small[j][l] - factor * small[i][l]
+                for b in column:
+                    column[b][j] = column[b][j] - factor * column[b][i]
+            row[i] = row[i] * inverse
+        for b in column:
+            for i in span:
+                below = column[b][i]
+                if b == home:
+                    below = jnp.where(sub > at + i, below, 0.0)
+                blocks[b] = blocks[b] - below * row[i]
     out = []
     for b in range(8):
         diagonal = jnp.sum(jnp.where(lane == sub + 8 * b, blocks[b], 0.0), axis=1, keepdims=True)
@@ -343,7 +359,12 @@
         pt[k] = pfull[k // 2, k % 2].T
         right += dot(pt[k], ev[k * FEAT : (k + 1) * FEAT, :])
         gram += dot(pt[k], pfull[k // 2, k % 2])
-    linv = inverse_factor(fold(gram[0:RANK] + gram[RANK:]))
+    def left(owner):
+        return dot(pt[owner], at[owner])
+
+    ap = left(t)
+    for owner in (sib, down, up, odown, oup, far):
+        ap += left(owner)
 
     for i in range(0, CUTS, 2):
         for h in range(2):
@@ -355,9 +376,7 @@
         r = pl.ds(pl.multiple_of(k * STEP, STEP), STEP)
         res[r, :] = (res[r, :].astype(F32) + proj[r, :] - tch[r, :].astype(F32)).astype(BF16)
 
-    ap = dot(pt[0], at[0])
-    for k in range(1, TP):
-        ap += dot(pt[k], at[k])
+    ap += left(ofar)
     ap = ap[0:RANK] + ap[RANK:]
     ap_high = ap.astype(BF16).astype(F32)
     ap_cat = jnp.concatenate([ap_high, ap - ap_high], axis=0).astype(BF16)
@@ -373,16 +392,21 @@
     send_dp(11, lambda peer: r_send.at[pl.ds(peer * PER, PER)], r_recv.at[d], r_recv.at[pl.ds(0, DP - 1)])
 
     def stored(k):
-        r = pl.ds(pl.multiple_of(k * 2 * FEAT, 2 * FEAT), 2 * FEAT)
+        r = pl.ds(k * 2 * FEAT, 2 * FEAT)
         return pltpu.make_async_copy(ev.at[r], m_hbm.at[r], out_sem.at[k])
 
     def matrix(k):
-        r = pl.ds(pl.multiple_of(k * 2 * FEAT, 2 * FEAT), 2 * FEAT)
+        r = pl.ds(k * 2 * FEAT, 2 * FEAT)
         grad = dot(at[pl.ds(2 * k, 2)].reshape(2 * FEAT, TOK), res[...]) * (1.0 / 32.0)
         ev[r, :] = (grad + ev[r, :].astype(F32)).astype(BF16)
         stored(k).start()
 
-    pl.loop(0, 2)(matrix)
+    matrix(0)
+    linv = inverse_factor(fold(gram[0:RANK] + gram[RANK:]))
+    lhigh = linv.astype(BF16).astype(F32)
+    lcat = split(linv)
+    ltcat = jnp.concatenate([lhigh.T[0:RANK], (linv - lhigh).T[0:RANK]], axis=1).astype(BF16)
+    matrix(1)
 
     wait_all(11)
     total = r_recv[0]
@@ -392,12 +416,8 @@
     send_dp(12, lambda peer: r_full.at[pl.ds(d * PER, PER)], r_full.at[pl.ds(d * PER, PER)],
             r_full.at[pl.ds(0, TILES - PER)])
 
-    pl.loop(2, 4)(matrix)
-    lhigh = linv.astype(BF16).astype(F32)
-    lcat = split(linv)
-    lhigh2 = lhigh.T
-    ltcat = jnp.concatenate([lhigh2[0:RANK], (linv - lhigh).T[0:RANK]], axis=1).astype(BF16)
-
+    matrix(2)
+    matrix(3)
     wait_all(12)
     summed = jnp.concatenate(
         [jnp.concatenate([r_full[i * 5 + j] for j in range(5)], axis=1) for i in range(8)], axis=0
@@ -416,8 +436,7 @@
         copy.wait_send()
     copy_p.wait()
 
-    @pl.loop(0, 4)
-    def _(k):
+    for k in range(4):
         stored(k).wait()
 
 

time: 88.2 us -> 79.7 us (0.904)
  Pallas kernels: 87.3 us -> 78.8 us
    pallas_call x1, Pallas kernels: 80.5 us -> 72 us  [per_device(): pl.pallas_call(main_kernel, name='gather_and_factors', out_shape=(jax.Sha...]
where the time goes in v4:
time: 79.7 us; the launch traced here: 79.6 us
  Pallas kernels  78.8 us (99%)
  between operations  0.8 us (1%)
    pallas_call x1, Pallas kernels, per_device(): pl.pallas_call(main_kernel, name='gather_and_factors', out_shape=(jax.Sha...  72 us
    pallas_call x1, Pallas kernels, per_device(): pl.pallas_call(write_kernel, name='write_error', out_shape=(jax.ShapeDtyp...  6.83 us

profile of v4, /device:TPU:0, one launch (start us, length us, event | category | flops | bytes accessed | tf_op | source)
XLA Modules:
  0.0 79.6 jit_solution(7501470470129485218)
XLA Ops:
  0.6 72.0 %gather_and_factors.1 = (bf16[4096,640]{1,0:T(8,128)(2,1)}, bf16[4,2,512,128]{3,2,1,0:T(8,128)(2,1)}, bf16[256,640]{1,0:T(8,128)(2,1)}, f32[64,640]{1,0:T(8,128)}) custom-call(bf16[1024,512]{1,0:T(8,128)(2,1)} %a_hbm.1, bf16[1024,640]{1,0:T(8,128)(2,1)} %res_hbm.1, bf16[1024,640]{1,0:T(8,128)(2,1)} %tch_hbm.1, bf16[8,512,640]{2,1,0:T(8,128)(2,1)} %bitcast.5, ...), custom_call_target="tpu_custom_call" | custom-call | tf_op jit(solution)/shard_map/gather_and_factors/pallas_call | solution.py:486
  72.6 6.8 %write_error.1 = (bf16[4096,640]{1,0:T(8,128)(2,1)}, f32[64,640]{1,0:T(8,128)}) custom-call(bf16[4096,640]{1,0:T(8,128)(2,1)} %get-tuple-element.8.m_hbm, bf16[4,2,512,128]{3,2,1,0:T(8,128)(2,1)} %get-tuple-element.9.p_hbm, bf16[256,640]{1,0:T(8,128)(2,1)} %get-tuple-element.10.coef_ref, f32[64,640]{1,0:T(8,128)} %get-tuple-element.11.qt_ref), custom_call_target="tpu_custom_call" | custom-call | tf_op jit(solution)/shard_map/write_error/pallas_call | solution.py:543

commit v5 on v4

--- a/solution.py
+++ b/solution.py
@@ -17,7 +17,7 @@
 GROUP = 4
 CUT = HALF // CUTS
 TILES = 48
-W2, W3 = 1, 1
+W2, W3 = 2, 1
 
 
 def dot(a, b):
@@ -84,7 +84,7 @@
 
 def main_kernel(
     a_hbm, res_hbm, tch_hbm, w_hbm, e_hbm, qt_ref,
-    m_hbm, p_hbm, coef_ref, qnext_ref,
+    m_ref, p_ref, coef_ref, qnext_ref,
     abuf, at, wv, ev, res, tch, proj, wblk, qcat, xq,
     wq_send, wq_recv, wq_full, dq_send, dq_recv, dq_full,
     pa_send, pa_recv, eq_send, e0_recv, e1_send, e_recv, e2_send, e2_recv, pfull, pt,
@@ -272,23 +272,6 @@
     for h in range(2):
         arrived(sib, h, 0, CUTS)
     take(sib, 0, TOK)
-    for owner, h in ((down, 0), (up, 1)):
-        for i in range(CUTS):
-            arrived(owner, h, i)
-        ag(owner, h, 0, sib, None, CUTS)
-        take(owner, h * HALF, HALF)
-
-    wait_all(5)
-
-    @pl.loop(0, 4)
-    def _(k):
-        total = e_recv[0, k].astype(F32)
-        for j in range(1, DP):
-            total += e_recv[j, k].astype(F32)
-        e2_send[k] = split(fold(total))
-
-    e2_recv[y] = e2_send[y]
-
     wait_all(3)
     total = dq_recv[0].astype(F32)
     for k in range(1, TP):
@@ -296,11 +279,25 @@
     dq_full[tokens(t), :] = split(fold(total))
     send_tp(4, lambda peer: dq_full.at[tokens(t)], dq_full.at[tokens(t)], dq_full.at[pl.ds(0, TOK - TOKP)])
 
+    wait_all(5)
+
+    @pl.loop(0, 4)
+    def _(k):
+        total = e_recv[0, k].astype(F32)
+        for j in range(1, DP):
+            total += e_recv[j, k].astype(F32)
+        e2_send[k] = split(fold(total))
+
+    e2_recv[y] = e2_send[y]
+
     send_y(6, lambda peer: e2_send.at[peer], e2_recv.at[y], e2_recv.at[pl.ds(0, 3)])
     own(1, range(W2, CUTS))
+    for owner, h in ((down, 0), (up, 1)):
+        for i in range(CUTS):
+            arrived(owner, h, i)
     pass_on(range(0, W3))
-    for owner, h in ((odown, 0), (oup, 1)):
-        arrived(owner, h, 0, CUTS)
+    for owner, h in ((down, 0), (up, 1)):
+        ag(owner, h, 0, sib, None, CUTS)
         take(owner, h * HALF, HALF)
 
     wait_all(4)
@@ -308,6 +305,10 @@
     pa_send[...] = split(fold(part))
     pa_recv[d] = pa_send[mine, :]
     send_dp(7, lambda peer: pa_send.at[piece(peer)], pa_recv.at[d], pa_recv.at[pl.ds(0, DP - 1)])
+
+    for owner, h in ((odown, 0), (oup, 1)):
+        arrived(owner, h, 0, CUTS)
+        take(owner, h * HALF, HALF)
 
     wait_all(6)
     wait_all(7)
@@ -336,6 +337,14 @@
         arrived(owner, h, 0, CUTS)
         take(owner, h * HALF, HALF)
 
+    def far_pieces(i):
+        for h in range(2):
+            arrived(far, h, i)
+            arrived(far, h, i + 1)
+            ag(far, h, i, sib, None, 2)
+
+    far_pieces(0)
+
     @pl.loop(1, DP)
     def _(k):
         source = lax.rem(d + DP - k, DP)
@@ -343,22 +352,16 @@
         pltpu.make_async_copy(block, block, p_recv.at[source]).wait()
         remote(10, block, block, {"tp": sib})
 
-    for i in range(0, CUTS, 2):
-        for h in range(2):
-            arrived(far, h, i)
-            arrived(far, h, i + 1)
-            ag(far, h, i, sib, None, 2)
+    far_pieces(2)
     take(far, 0, TOK)
 
     wait_all(10)
-    copy_p = pltpu.make_async_copy(pfull, p_hbm, out_sem.at[TP])
+    copy_p = pltpu.make_async_copy(pfull, p_ref, out_sem)
     copy_p.start()
     right = jnp.zeros((128, COLS), F32)
-    gram = jnp.zeros((128, 128), F32)
     for k in range(TP):
         pt[k] = pfull[k // 2, k % 2].T
         right += dot(pt[k], ev[k * FEAT : (k + 1) * FEAT, :])
-        gram += dot(pt[k], pfull[k // 2, k % 2])
     def left(owner):
         return dot(pt[owner], at[owner])
 
@@ -391,17 +394,15 @@
     r_recv[d] = r_send[pl.ds(d * PER, PER)]
     send_dp(11, lambda peer: r_send.at[pl.ds(peer * PER, PER)], r_recv.at[d], r_recv.at[pl.ds(0, DP - 1)])
 
-    def stored(k):
-        r = pl.ds(k * 2 * FEAT, 2 * FEAT)
-        return pltpu.make_async_copy(ev.at[r], m_hbm.at[r], out_sem.at[k])
-
     def matrix(k):
         r = pl.ds(k * 2 * FEAT, 2 * FEAT)
         grad = dot(at[pl.ds(2 * k, 2)].reshape(2 * FEAT, TOK), res[...]) * (1.0 / 32.0)
-        ev[r, :] = (grad + ev[r, :].astype(F32)).astype(BF16)
-        stored(k).start()
+        m_ref[r, :] = (grad + ev[r, :].astype(F32)).astype(BF16)
 
     matrix(0)
+    gram = dot(pt[0], pfull[0, 0])
+    for k in range(1, TP):
+        gram += dot(pt[k], pfull[k // 2, k % 2])
     linv = inverse_factor(fold(gram[0:RANK] + gram[RANK:]))
     lhigh = linv.astype(BF16).astype(F32)
     lcat = split(linv)
@@ -436,46 +437,32 @@
         copy.wait_send()
     copy_p.wait()
 
-    for k in range(4):
-        stored(k).wait()
-
 
 CHUNKS = 8
 CHUNK = ROWS // CHUNKS
 
 
-def write_kernel(m_hbm, p_hbm, coef_ref, qt_ref, out_hbm, qout_ref, m, p, out, m_sem, p_sem, out_sem):
-    def load(k):
-        r = pl.ds(pl.multiple_of(k * CHUNK, CHUNK), CHUNK)
-        return (
-            pltpu.make_async_copy(m_hbm.at[r], m.at[r], m_sem.at[k]),
-            pltpu.make_async_copy(p_hbm.at[k // 2, lax.rem(k, 2)], p.at[r], p_sem.at[k]),
-        )
-
+def write_kernel(m_ref, p_ref, coef_ref, qt_ref, out_hbm, qout_hbm, out, out_sem):
     def store(k):
         r = pl.ds(pl.multiple_of(k * CHUNK, CHUNK), CHUNK)
         return pltpu.make_async_copy(out.at[r], out_hbm.at[r], out_sem.at[k])
 
+    store_q = pltpu.make_async_copy(qt_ref, qout_hbm, out_sem.at[CHUNKS])
+    store_q.start()
+
     @pl.loop(0, CHUNKS)
     def _(k):
-        for copy in load(k):
-            copy.start()
-
-    qout_ref[...] = qt_ref[...]
+        r = pl.ds(pl.multiple_of(k * CHUNK, CHUNK), CHUNK)
+        cat = p_ref[k // 2, lax.rem(k, 2)]
+        approx = dot(jnp.concatenate([cat, cat], axis=1), coef_ref[...])
+        out[r, :] = (m_ref[r, :].astype(F32) - approx).astype(BF16)
+        store(k).start()
 
     @pl.loop(0, CHUNKS)
     def _(k):
-        for copy in load(k):
-            copy.wait()
-        r = pl.ds(pl.multiple_of(k * CHUNK, CHUNK), CHUNK)
-        cat = p[r, :]
-        approx = dot(jnp.concatenate([cat, cat], axis=1), coef_ref[...])
-        out[r, :] = (m[r, :].astype(F32) - approx).astype(BF16)
-        store(k).start()
-
-    @pl.loop(0, CHUNKS)
-    def _(k):
         store(k).wait()
+
+    store_q.wait()
 
 
 def per_device(attn_out, residual_in, teacher, out_weight, error_buf, q_start):
@@ -487,13 +474,13 @@
         main_kernel,
         name="gather_and_factors",
         out_shape=(
-            jax.ShapeDtypeStruct((ROWS, COLS), BF16),
-            jax.ShapeDtypeStruct((4, 2, FEAT, 128), BF16),
-            jax.ShapeDtypeStruct((256, COLS), BF16),
-            jax.ShapeDtypeStruct((RANK, COLS), F32),
+            V((ROWS, COLS), BF16),
+            V((4, 2, FEAT, 128), BF16),
+            V((256, COLS), BF16),
+            V((RANK, COLS), F32),
         ),
         in_specs=[any_space] * 5 + [vmem],
-        out_specs=(any_space, any_space, vmem, vmem),
+        out_specs=(vmem, vmem, vmem, vmem),
         scratch_shapes=[
             V((TP, TOK, FEAT), BF16),
             V((TP, FEAT, TOK), BF16),
@@ -530,10 +517,10 @@
             S((13,)),
             S((13,)),
             S((DP,)),
-            S((TP + 1,)),
+            S,
         ],
         compiler_params=pltpu.CompilerParams(
-            collective_id=0, has_side_effects=True, vmem_limit_bytes=60 * 2**20
+            collective_id=0, has_side_effects=True, vmem_limit_bytes=50 * 2**20
         ),
     )(
         attn_out, residual_in, teacher,
@@ -547,17 +534,13 @@
             jax.ShapeDtypeStruct((ROWS, COLS), BF16),
             jax.ShapeDtypeStruct((RANK, COLS), F32),
         ),
-        in_specs=[any_space, any_space, vmem, vmem],
-        out_specs=(any_space, vmem),
+        in_specs=[vmem] * 4,
+        out_specs=(any_space, any_space),
         scratch_shapes=[
             V((ROWS, COLS), BF16),
-            V((ROWS, 128), BF16),
-            V((ROWS, COLS), BF16),
-            S((CHUNKS,)),
-            S((CHUNKS,)),
-            S((CHUNKS,)),
+            S((CHUNKS + 1,)),
         ],
-        compiler_params=pltpu.CompilerParams(vmem_limit_bytes=60 * 2**20),
+        compiler_params=pltpu.CompilerParams(vmem_limit_bytes=16 * 2**20),
     )(m, p, coef, qt)
     return error_next[None], q_next.T
 

time: 79.7 us -> 74.9 us (0.940)
  Pallas kernels: 78.8 us -> 74 us
    pallas_call x1, Pallas kernels: 6.83 us -> 3.9 us  [per_device(): pl.pallas_call(write_kernel, name='write_error', out_shape=(jax.ShapeDtyp...]
    pallas_call x1, Pallas kernels: 72 us -> 70.1 us  [per_device(): pl.pallas_call(main_kernel, name='gather_and_factors', out_shape=(V((ROWS...]
where the time goes in v5:
time: 74.9 us; the launch traced here: 74.8 us
  Pallas kernels  74 us (99%)
  between operations  0.8 us (1%)
    pallas_call x1, Pallas kernels, per_device(): pl.pallas_call(main_kernel, name='gather_and_factors', out_shape=(V((ROWS...  70.1 us
    pallas_call x1, Pallas kernels, per_device(): pl.pallas_call(write_kernel, name='write_error', out_shape=(jax.ShapeDtyp...  3.9 us

profile of v5, /device:TPU:0, one launch (start us, length us, event | category | flops | bytes accessed | tf_op | source)
XLA Modules:
  0.0 74.8 jit_solution(17042577164732068276)
XLA Ops:
  0.6 70.1 %gather_and_factors.1 = (bf16[4096,640]{1,0:T(8,128)(2,1)S(1)}, bf16[4,2,512,128]{3,2,1,0:T(8,128)(2,1)S(1)}, bf16[256,640]{1,0:T(8,128)(2,1)S(1)}, f32[64,640]{1,0:T(8,128)S(1)}) custom-call(bf16[1024,512]{1,0:T(8,128)(2,1)} %a_hbm.1, bf16[1024,640]{1,0:T(8,128)(2,1)} %res_hbm.1, bf16[1024,640]{1,0:T(8,128)(2,1)} %tch_hbm.1, bf16[8,512,640]{2,1,0:T(8,128)(2,1)} %bitcast.5, ...), custom_call_target="tpu_custom_call" | custom-call | tf_op jit(solution)/shard_map/gather_and_factors/pallas_call | solution.py:473
  70.7 3.9 %write_error.1 = (bf16[4096,640]{1,0:T(8,128)(2,1)}, f32[64,640]{1,0:T(8,128)}) custom-call(bf16[4096,640]{1,0:T(8,128)(2,1)S(1)} %get-tuple-element.8.m_ref, bf16[4,2,512,128]{3,2,1,0:T(8,128)(2,1)S(1)} %get-tuple-element.9.p_ref, bf16[256,640]{1,0:T(8,128)(2,1)S(1)} %get-tuple-element.10.coef_ref, f32[64,640]{1,0:T(8,128)S(1)} %get-tuple-element.11.qt_ref), custom_call_target="tpu_custom_call" | custom-call | tf_op jit(solution)/shard_map/write_error/pallas_call | solution.py:530

commit v6 on v5

--- a/solution.py
+++ b/solution.py
@@ -106,9 +106,10 @@
     load_res = pltpu.make_async_copy(res_hbm, res, load_sem.at[3])
     load_tch = pltpu.make_async_copy(tch_hbm, tch, load_sem.at[4])
     load_w = pltpu.make_async_copy(w_hbm, wv, load_sem.at[5])
-    for load in (load_blk, load_res, load_tch, load_e, load_a, load_w):
+    for load in (load_blk, load_e, load_a, load_res, load_tch, load_w):
         load.start()
 
+    STEP = 512
     barrier = pltpu.get_barrier_semaphore()
 
     @pl.loop(1, TP)
@@ -127,15 +128,6 @@
     part = dot(wblk[...].reshape(TP * PIECE, COLS), qcat[...])
     wq_send[...] = split(fold(part)).reshape(TP, PIECE, 128)
     wq_recv[t] = wq_send[t]
-
-    load_res.wait()
-    load_tch.wait()
-    STEP = 512
-
-    @pl.loop(0, TOK // STEP)
-    def _(k):
-        r = pl.ds(pl.multiple_of(k * STEP, STEP), STEP)
-        xq[r, :] = dot(res[r, :], qcat[...]) - dot(tch[r, :], qcat[...])
 
     pl.semaphore_wait(barrier, TP - 1 + DP - 1)
 
@@ -236,6 +228,14 @@
 
     e_recv[d] = e1_send[:, mine, :]
     send_dp(5, lambda peer: e1_send.at[:, piece(peer)], e_recv.at[d], e_recv.at[pl.ds(0, DP - 1)])
+
+    load_res.wait()
+    load_tch.wait()
+
+    @pl.loop(0, TOK // STEP)
+    def _(k):
+        r = pl.ds(pl.multiple_of(k * STEP, STEP), STEP)
+        xq[r, :] = dot(res[r, :], qcat[...]) - dot(tch[r, :], qcat[...])
 
     load_a.wait()
     load_w.wait()

time: 74.9 us -> 74.9 us (level)
  no operation moved by 1% of the time
where the time goes in v6:
time: 74.9 us; the launch traced here: 74.8 us
  Pallas kernels  74 us (99%)
  between operations  0.8 us (1%)
    pallas_call x1, Pallas kernels, per_device(): pl.pallas_call(main_kernel, name='gather_and_factors', out_shape=(V((ROWS...  70.1 us
    pallas_call x1, Pallas kernels, per_device(): pl.pallas_call(write_kernel, name='write_error', out_shape=(jax.ShapeDtyp...  3.9 us

profile of v6, /device:TPU:0, one launch (start us, length us, event | category | flops | bytes accessed | tf_op | source)
XLA Modules:
  0.0 74.8 jit_solution(14174021127586861250)
XLA Ops:
  0.6 70.1 %gather_and_factors.1 = (bf16[4096,640]{1,0:T(8,128)(2,1)S(1)}, bf16[4,2,512,128]{3,2,1,0:T(8,128)(2,1)S(1)}, bf16[256,640]{1,0:T(8,128)(2,1)S(1)}, f32[64,640]{1,0:T(8,128)S(1)}) custom-call(bf16[1024,512]{1,0:T(8,128)(2,1)} %a_hbm.1, bf16[1024,640]{1,0:T(8,128)(2,1)} %res_hbm.1, bf16[1024,640]{1,0:T(8,128)(2,1)} %tch_hbm.1, bf16[8,512,640]{2,1,0:T(8,128)(2,1)} %bitcast.5, ...), custom_call_target="tpu_custom_call" | custom-call | tf_op jit(solution)/shard_map/gather_and_factors/pallas_call | solution.py:473
  70.7 3.9 %write_error.1 = (bf16[4096,640]{1,0:T(8,128)(2,1)}, f32[64,640]{1,0:T(8,128)}) custom-call(bf16[4096,640]{1,0:T(8,128)(2,1)S(1)} %get-tuple-element.8.m_ref, bf16[4,2,512,128]{3,2,1,0:T(8,128)(2,1)S(1)} %get-tuple-element.9.p_ref, bf16[256,640]{1,0:T(8,128)(2,1)S(1)} %get-tuple-element.10.coef_ref, f32[64,640]{1,0:T(8,128)S(1)} %get-tuple-element.11.qt_ref), custom_call_target="tpu_custom_call" | custom-call | tf_op jit(solution)/shard_map/write_error/pallas_call | solution.py:530
